TPU v7x, 256 devices: a whole 4x4x8 slice. The times are simulated.
256 devices in a mesh: tiles: 64 (over x, z_lo, y), dp: 4 (over z_hi, core).
Axes of the slice: x: 4, y: 4, z: 8 (z_hi: 2, z_lo: 4; z = z_hi * 4 + z_lo), core: 2. Of those that a mesh axis runs over, the one named last changes fastest.
Arguments:
- sea_state: bfloat16 [4, 64, 64, 64, 128], P('dp', 'tiles'), may hold values from -6 to 6
- cotangent: bfloat16 [4, 64, 64, 64, 128], P('dp', 'tiles'), may hold values from -6 to 6
- kernel: float32 [7, 7, 128], replicated, may hold values from -0.875 to 0.875
- conv_bias: float32 [128], replicated, may hold values from -4 to 4
- ln_gain: float32 [128], replicated, may hold values from 0.25 to 1.75
- ln_bias: float32 [128], replicated, may hold values from -3 to 3
- w_in: bfloat16 [128, 512], replicated, may hold values from -0.5 to 0.5
- b_in: float32 [512], replicated, may hold values from -3 to 3
- w_out: bfloat16 [512, 128], replicated, may hold values from -0.25 to 0.25
- b_out: float32 [128], replicated, may hold values from -3 to 3
- layer_scale: float32 [128], replicated, may hold values from 0.5 to 1.5
- tile_deal: int32 [64], replicated, may hold values from 0 to 63, each once
- adjacency: int32 [64, 8], replicated, may hold values from -1 to 63, as said below
Outputs:
- out_field: bfloat16 [4, 64, 64, 64, 128], P('dp', 'tiles')
- grad_field: bfloat16 [4, 64, 64, 64, 128], P('dp', 'tiles')
- grad_kernel: float32 [7, 7, 128], replicated
- grad_conv_bias: float32 [128], replicated
- grad_ln_gain: float32 [128], replicated
- grad_ln_bias: float32 [128], replicated
- grad_w_in: float32 [128, 512], replicated
- grad_b_in: float32 [512], replicated
- grad_w_out: float32 [512, 128], replicated
- grad_b_out: float32 [128], replicated
- grad_layer_scale: float32 [128], replicated
Inputs may be any that keep to these rules, and one draw needn't show every extreme that they name: The window is 4 tile rows by 32 tile columns, of which 64 are wet, numbered in row order; neighbours wrap in longitude and not in latitude; adjacency is symmetric, and no two directions of one tile name the same tile.
All inputs are finite; a program needn't handle non-finite values.
Results may differ from a plain program's by a relative error of at most 0.0072.
Values may be sent and summed in bfloat16 or wider, within the bound.
A program may use at most 128 MiB of HBM per device.

v0:
```python
import math

import jax
import jax.numpy as jnp
from jax import lax
from jax.sharding import PartitionSpec as P


def frame_of(own_tile):
    return jnp.stack(
        [
            own_tile[:, -3:],
            own_tile[:, :3],
            jnp.swapaxes(own_tile[:, :, -3:], 1, 2),
            jnp.swapaxes(own_tile[:, :, :3], 1, 2),
        ]
    )


def expand(frame):
    strip_len = frame.shape[-2]
    bottom = frame[..., 0, :, :, :, :]
    top_rows = frame[..., 1, :, :, :, :]

    def pad_corner(piece):
        return jnp.pad(piece, [(0, 0)] * (piece.ndim - 2) + [(0, strip_len - 3), (0, 0)])

    corners = [
        pad_corner(bottom[..., -3:, :]),
        pad_corner(bottom[..., :3, :]),
        pad_corner(top_rows[..., -3:, :]),
        pad_corner(top_rows[..., :3, :]),
    ]
    return jnp.concatenate([frame, jnp.stack(corners, axis=-5)], axis=-5)


def assemble(own_tile, halo_rows):
    west_cells = jnp.swapaxes(halo_rows[2], 1, 2)
    east_cells = jnp.swapaxes(halo_rows[3], 1, 2)
    middle = jnp.concatenate([west_cells, own_tile, east_cells], axis=2)
    upper_band = jnp.concatenate(
        [halo_rows[4][:, :, :3], halo_rows[0], halo_rows[5][:, :, :3]], axis=2
    )
    lower_band = jnp.concatenate(
        [halo_rows[6][:, :, :3], halo_rows[1], halo_rows[7][:, :, :3]], axis=2
    )
    return jnp.concatenate([upper_band, middle, lower_band], axis=1)


def depthwise(padded, kernel, tile_size, flipped):
    taps = kernel.shape[0]
    total = jnp.zeros(padded.shape[:1] + (tile_size, tile_size, padded.shape[-1]), jnp.float32)
    for i in range(taps):
        band = padded[:, i : i + tile_size]
        row_sum = None
        for j in range(taps):
            weight = kernel[taps - 1 - i, taps - 1 - j] if flipped else kernel[i, j]
            term = weight * band[:, :, j : j + tile_size].astype(jnp.float32)
            row_sum = term if row_sum is None else row_sum + term
        total = total + row_sum
    return total


def local_pass(
    own_tile,
    padded,
    upstream,
    kernel,
    conv_bias,
    ln_gain,
    ln_bias,
    w_in,
    b_in,
    w_out,
    b_out,
    layer_scale,
):
    tile_size = own_tile.shape[1]
    channels = own_tile.shape[-1]
    convolved = depthwise(padded, kernel, tile_size, False) + conv_bias
    row_mean = jnp.mean(convolved, -1, keepdims=True)
    centred = convolved - row_mean
    inv_std = lax.rsqrt(jnp.mean(centred * centred, -1, keepdims=True) + 1e-06)
    whitened = centred * inv_std
    normed = (whitened * ln_gain + ln_bias).astype(jnp.bfloat16).reshape(-1, channels)
    pre_act = jnp.dot(normed, w_in, preferred_element_type=jnp.float32) + b_in
    act_full, gelu_back = jax.vjp(jax.nn.gelu, pre_act)
    activation = act_full.astype(jnp.bfloat16)
    branch_out = jnp.dot(activation, w_out, preferred_element_type=jnp.float32) + b_out
    flat_input = own_tile.reshape(-1, channels).astype(jnp.float32)
    result = (flat_input + layer_scale * branch_out).astype(jnp.bfloat16).reshape(own_tile.shape)
    up_rows = upstream.reshape(-1, channels).astype(jnp.float32)
    grad_out = up_rows * layer_scale
    grad_out16 = grad_out.astype(jnp.bfloat16)
    grad_scale = jnp.sum(up_rows * branch_out, 0)
    grad_bout = jnp.sum(grad_out, 0)
    grad_wout = jnp.dot(activation.T, grad_out16, preferred_element_type=jnp.float32)
    grad_act = jnp.dot(grad_out16, w_out.T, preferred_element_type=jnp.float32)
    grad_pre = gelu_back(grad_act)[0]
    grad_pre16 = grad_pre.astype(jnp.bfloat16)
    grad_bin = jnp.sum(grad_pre, 0)
    grad_win = jnp.dot(normed.T, grad_pre16, preferred_element_type=jnp.float32)
    grad_normed = jnp.dot(grad_pre16, w_in.T, preferred_element_type=jnp.float32).reshape(
        whitened.shape
    )
    grad_gain = jnp.sum(grad_normed * whitened, (0, 1, 2))
    grad_lnb = jnp.sum(grad_normed, (0, 1, 2))
    grad_white = grad_normed * ln_gain
    grad_conv = inv_std * (
        grad_white
        - jnp.mean(grad_white, -1, keepdims=True)
        - whitened * jnp.mean(grad_white * whitened, -1, keepdims=True)
    )
    grad_cbias = jnp.sum(grad_conv, (0, 1, 2))
    return (
        result,
        grad_conv.astype(jnp.bfloat16),
        (grad_cbias, grad_gain, grad_lnb, grad_win, grad_bin, grad_wout, grad_bout, grad_scale),
    )


def tap_grads(padded, grad_conv16, kernel):
    tile_size = grad_conv16.shape[1]
    taps = kernel.shape[0]
    rows_list = []
    for i in range(taps):
        for j in range(taps):
            rows_list.append(
                jnp.sum(
                    padded[:, i : i + tile_size, j : j + tile_size].astype(jnp.float32)
                    * grad_conv16.astype(jnp.float32),
                    (0, 1, 2),
                )
            )
    return jnp.stack(rows_list).reshape(taps, taps, -1)


def neighbours(tile_deal, adjacency):
    my_index = lax.axis_index("tiles")
    near_tiles = adjacency[tile_deal[my_index]]
    is_wet = near_tiles >= 0
    matches = tile_deal[None, :] == near_tiles[:, None]
    source = jnp.sum(
        matches.astype(jnp.int32) * jnp.arange(tile_deal.shape[0], dtype=jnp.int32)[None, :], 1
    )
    return (matches, source, is_wet)


def by_frames(own_tile, source, is_wet, second):
    frame = frame_of(own_tile)[None]

    def collect(incoming):
        piece_rows = incoming.shape[0]
        rank_ids = jnp.arange(piece_rows, dtype=jnp.int32)
        chosen = ((source[:, None] == rank_ids[None, :]) & is_wet[:, None]).astype(incoming.dtype)
        return jnp.einsum(
            "jn,njsrtc->jsrtc", chosen, expand(incoming), preferred_element_type=jnp.float32
        )

    if second:
        gathered = collect(lax.all_gather(frame, "tiles", axis=0, tiled=True))
    else:
        gathered = collect(lax.all_gather(frame, "tiles", axis=0, tiled=True))
    return gathered.astype(own_tile.dtype)


def fetch(own_tile, source, is_wet, second):
    return by_frames(own_tile, source, is_wet, second)


def on_device(
    sea_state,
    cotangent,
    kernel,
    conv_bias,
    ln_gain,
    ln_bias,
    w_in,
    b_in,
    w_out,
    b_out,
    layer_scale,
    tile_deal,
    adjacency,
):
    own_tile = sea_state[:, 0]
    upstream = cotangent[:, 0]
    tile_size = own_tile.shape[1]
    matches, source, is_wet = neighbours(tile_deal, adjacency)
    padded = assemble(own_tile, fetch(own_tile, source, is_wet, False))
    result, grad_conv16, grad_parts = local_pass(
        own_tile,
        padded,
        upstream,
        kernel,
        conv_bias,
        ln_gain,
        ln_bias,
        w_in,
        b_in,
        w_out,
        b_out,
        layer_scale,
    )
    padded_grad = assemble(grad_conv16, fetch(grad_conv16, source, is_wet, True))
    grad_input = (
        upstream.astype(jnp.float32) + depthwise(padded_grad, kernel, tile_size, True)
    ).astype(jnp.bfloat16)
    grad_taps = tap_grads(padded, grad_conv16, kernel)
    everything = lax.psum(
        (
            grad_parts[0],
            grad_parts[1],
            grad_parts[2],
            grad_parts[3],
            grad_parts[4],
            grad_parts[5],
            grad_parts[6],
            grad_parts[7],
            grad_taps,
        ),
        ("tiles", "dp"),
    )
    summed = tuple(everything[:8])
    grad_taps = everything[8]
    factor = 1.0 / math.sqrt(
        own_tile.shape[0] * tile_size * tile_size * lax.axis_size("tiles") * lax.axis_size("dp")
    )
    scaled = [part * factor for part in summed]
    return (
        result[:, None],
        grad_input[:, None],
        grad_taps * factor,
        scaled[0],
        scaled[1],
        scaled[2],
        scaled[3],
        scaled[4],
        scaled[5],
        scaled[6],
        scaled[7],
    )


def solution(mesh):
    in_specs = (
        P("dp", "tiles", None, None, None),
        P("dp", "tiles", None, None, None),
        P(),
        P(),
        P(),
        P(),
        P(),
        P(),
        P(),
        P(),
        P(),
        P(),
        P(),
    )
    out_specs = (
        P("dp", "tiles", None, None, None),
        P("dp", "tiles", None, None, None),
        P(),
        P(),
        P(),
        P(),
        P(),
        P(),
        P(),
        P(),
        P(),
    )
    return jax.shard_map(
        on_device, mesh=mesh, in_specs=in_specs, out_specs=out_specs, check_vma=False
    )
```

profile of v0, /device:TPU:8, one launch (start us, length us, event | category | flops | bytes accessed | tf_op | source)
XLA Modules:
  0.0 1198.3 jit_solution(16520183530850739334)
XLA Ops:
  7.2 0.9 fusion.146
  8.1 1.0 slice_bitcast_fusion.9
  9.2 0.2 pad_maximum_fusion.5
  9.5 0.7 copy.76
  10.3 1.2 dynamic_slice.6
  13.5 0.9 dynamic-slice_reduce_fusion
  14.3 0.8 select_reduce_fusion
  15.2 0.9 slice_bitcast_fusion.58
  16.2 1.0 slice_bitcast_fusion.60
  17.4 1.6 slice_bitcast_fusion.59
  19.1 365.7 %all-gather.5.cloned.1.call-done = bf16[256,1,3,64,128]{4,3,2,1,0:T(8,128)(2,1)} async-done(((bf16[4,1,3,64,128]{4,3,2,1,0:T(8,128)(2,1)}), bf16[256,1,3,64,128]{4,3,2,1,0:T(8,128)(2,1)}) %all-gather.5.cloned.1.call-update) | async-done | bytes 12582928 | tf_op jit(solution)/shard_map/all_gather | solution.py:163
  384.8 2.8 slice_bitcast_fusion.3
  387.6 13.0 %constant_dynamic-update-slice_fusion = bf16[64,8,1,3,64,128]{5,4,3,1,0,2:T(8,128)(2,1)} fusion(bf16[64,4,1,3,64,128]{5,4,3,1,0,2:T(8,128)(2,1)} %bitcast.263), kind=kLoop, calls=%fused_computation.308 | loop fusion | bytes 25165824
  400.7 2.5 bitcast_dynamic-update-slice_fusion.3
  403.2 3.8 slice_bitcast_fusion.2
  407.1 2.5 bitcast_dynamic-update-slice_fusion.2
  409.6 2.9 select_dynamic-update-slice_fusion.2
  412.5 24.4 %fusion.2 = f32[8,1,3,64,128]{4,1,3,2,0:T(1,128)S(1)} fusion(bf16[64,8,3,64,128]{4,3,2,1,0:T(8,128)(2,1)} %bitcast.18, pred[8,64,1,1,1]{1,0,2,3,4:T(8,128)(4,1)S(1)} %fusion.140), kind=kOutput, calls=%fused_computation.52 | convolution fusion | flops 25165824 | bytes 25952768 | tf_op jit(solution)/shard_map/jn,njsrtc->jsrtc/dot_general | solution.py:156
  437.2 1.0 copy-done.10
  438.2 3.6 maximum_maximum_fusion
  442.2 15.9 %fusion.143 = (f32[64,64]{1,0:T(8,128)S(1)}, f32[1,64,64,128]{3,2,1,0:T(8,128)S(1)}) fusion(f32[128]{0:T(128)S(1)} %copy-done.105, bf16[1,67,70,128]{3,2,1,0:T(8,128)(2,1)S(1)} %get-tuple-element.105, f32[128]{0:T(128)S(1)} %get-tuple-element.178, f32[128]{0:T(128)S(1)} %get-tuple-element.179, f32[128]{0:T(128)S(1)} %get-tuple-element.132, ...), kind=kLoop, calls=%fused_computation.378 | loop fusion | flops 87027712 | bytes 47326208 | tf_op jit(solution)/shard_map/reduce_sum | solution.py:81
  458.2 1.3 multiply_reduce_fusion.3
  459.5 1.3 add_convert_fusion
  460.9 3.3 multiply_convert_fusion
  464.2 2.7 fusion.121
  467.0 2.0 fusion.152
  468.9 7.2 fusion.151
  476.2 1.9 copy-done.9
  478.1 1.4 fusion.122
  479.6 5.3 fusion.141
  484.9 3.7 multiply_reduce_fusion.1
  488.7 6.9 fusion.117
  495.6 1.0 copy-done.6
  496.7 1.0 slice_bitcast_fusion.7
  497.8 0.2 pad_maximum_fusion.6
  498.0 0.7 copy.85
  498.8 2.3 fusion.119
  501.1 3.0 fusion.72
  504.1 4.0 fusion.116
  508.2 5.9 fusion.89
  514.2 4.3 stack.259
  518.5 4.0 multiply_reduce_fusion
  522.6 76.0 %all-reduce.4 = (f32[7,7,128]{2,1,0:T(8,128)S(1)}, f32[128]{0:T(128)S(1)}, f32[128]{0:T(128)S(1)}, f32[128]{0:T(128)S(1)}, f32[512]{0:T(512)S(1)}, /*index=5*/f32[128]{0:T(128)S(1)}, f32[128]{0:T(128)S(1)}) all-reduce(f32[7,7,128]{2,1,0:T(8,128)S(1)} %reshape.362, ...), channel_id=1, replica_groups=mesh['tiles'=64,'dp'=4] {'tiles','dp'}, use_global_device_ids=true, to_apply=%region_54.55 | all-reduce | flops 7424 | bytes 59392 | tf_op jit(solution)/shard_map/psum | solution.py:210
  598.6 0.5 broadcast_multiply_fusion.11
  599.1 0.5 broadcast_multiply_fusion.10
  599.6 0.5 broadcast_multiply_fusion.9
  600.1 0.5 broadcast_multiply_fusion.8
  600.6 0.5 broadcast_multiply_fusion.7
  601.2 0.6 broadcast_multiply_fusion.6
  601.7 0.6 broadcast_multiply_fusion.4
  602.3 145.9 %all-reduce.8.cloned.1.call-done = (f32[128,512]{1,0:T(8,128)}, f32[512,128]{1,0:T(8,128)}) async-done(((f32[128,512]{1,0:T(8,128)}, f32[512,128]{1,0:T(8,128)}), (f32[128,512]{1,0:T(8,128)}, f32[512,128]{1,0:T(8,128)})) %all-reduce.8.cloned.1.call-update) | async-done | bytes 524304 | tf_op jit(solution)/shard_map/psum | solution.py:210
  748.3 1.7 broadcast_multiply_fusion.1
  750.0 1.7 broadcast_multiply_fusion
  751.6 368.7 %all-gather.7.cloned.1.call-done = bf16[256,1,3,64,128]{4,3,2,1,0:T(8,128)(2,1)} async-done(((bf16[4,1,3,64,128]{4,3,2,1,0:T(8,128)(2,1)}), bf16[256,1,3,64,128]{4,3,2,1,0:T(8,128)(2,1)}) %all-gather.7.cloned.1.call-update) | async-done | bytes 12582928 | tf_op jit(solution)/shard_map/all_gather | solution.py:161
  1120.4 2.8 slice_bitcast_fusion.1
  1123.2 13.0 %constant_dynamic-update-slice_fusion.1 = bf16[64,8,1,3,64,128]{5,4,3,1,0,2:T(8,128)(2,1)} fusion(bf16[64,4,1,3,64,128]{5,4,3,1,0,2:T(8,128)(2,1)} %bitcast.257), kind=kLoop, calls=%fused_computation.309 | loop fusion | bytes 25165824
  1136.2 2.5 bitcast_dynamic-update-slice_fusion.1
  1138.7 3.8 slice_bitcast_fusion
  1142.6 2.5 bitcast_dynamic-update-slice_fusion
  1145.2 2.9 select_dynamic-update-slice_fusion
  1148.1 24.7 %fusion = bf16[8,1,3,64,128]{4,1,3,2,0:T(2,128)(2,1)S(1)} fusion(bf16[64,8,3,64,128]{4,3,2,1,0:T(8,128)(2,1)} %bitcast.89, pred[8,64,1,1,1]{1,0,2,3,4:T(8,128)(4,1)S(1)} %fusion.140), kind=kOutput, calls=%fused_computation.50 | convolution fusion | flops 25165824 | bytes 25559552 | tf_op jit(solution)/shard_map/jn,njsrtc->jsrtc/dot_general | solution.py:156
  1172.8 0.5 copy.112
  1174.0 0.6 maximum_maximum_fusion.2
  1175.2 16.3 %fusion.134 = bf16[1,1,64,64,128]{4,3,2,1,0:T(8,128)(2,1)} fusion(bf16[1,67,70,128]{3,2,1,0:T(8,128)(2,1)S(1)} %get-tuple-element.103, f32[128]{0:T(128)S(1)} %copy-done.33, f32[128]{0:T(128)S(1)} %copy-done.71, f32[128]{0:T(128)S(1)} %get-tuple-element.169, f32[128]{0:T(128)S(1)} %copy-done.27, f32[128]{0:T(128)S(1)} %copy-done.25, f32[128]{0:T(128)S(1)} %copy-done.23, ...), kind=kLoop, calls=%fused_computation.286 | loop fusion | flops 87556096 | bytes 47309312 | tf_op jit(solution)/shard_map/broadcast_in_dim | solution.py:232
  (266 shorter events, 2.1 us)
Async XLA Ops:
  7.2 453.6 %copy-start = (bf16[128,512]{1,0:T(8,128)(2,1)S(1)}, bf16[128,512]{1,0:T(8,128)(2,1)}, u32[]{:S(2)}) copy-start(bf16[128,512]{1,0:T(8,128)(2,1)} %param.19) | copy-start | bytes 393220
  7.2 377.6 %all-gather.5.cloned.1.call-start = ((), (), s32[]{:S(2)}) async-start(), calls=%async_computation | async-start | bytes 12779520 | tf_op jit(solution)/shard_map/all_gather | solution.py:163
  10.2 738.1 %all-reduce.8.cloned.1.call-start = ((), (), s32[]{:S(2)}) async-start(), calls=%async_computation.2 | async-start | bytes 1048576 | tf_op jit(solution)/shard_map/psum | solution.py:210
  16.1 425.6 %copy-start.16 = (f32[128]{0:T(128)}, f32[128]{0:T(128)S(1)}, u32[]{:S(2)}) copy-start(f32[128]{0:T(128)S(1)} %get-tuple-element.172) | copy-start | bytes 1540
  16.2 425.6 %copy-start.18 = (f32[128]{0:T(128)}, f32[128]{0:T(128)S(1)}, u32[]{:S(2)}) copy-start(f32[128]{0:T(128)S(1)} %get-tuple-element.173) | copy-start | bytes 1540
  16.2 425.6 %copy-start.20 = (f32[128]{0:T(128)}, f32[128]{0:T(128)S(1)}, u32[]{:S(2)}) copy-start(f32[128]{0:T(128)S(1)} %get-tuple-element.174) | copy-start | bytes 1540
  16.2 425.6 %copy-start.22 = (f32[128]{0:T(128)}, f32[128]{0:T(128)S(1)}, u32[]{:S(2)}) copy-start(f32[128]{0:T(128)S(1)} %get-tuple-element.175) | copy-start | bytes 1540
  16.2 425.6 %copy-start.24 = (f32[128]{0:T(128)}, f32[128]{0:T(128)S(1)}, u32[]{:S(2)}) copy-start(f32[128]{0:T(128)S(1)} %get-tuple-element.176) | copy-start | bytes 1540
  16.2 425.6 %copy-start.26 = (f32[128]{0:T(128)}, f32[128]{0:T(128)S(1)}, u32[]{:S(2)}) copy-start(f32[128]{0:T(128)S(1)} %get-tuple-element.177) | copy-start | bytes 1540
  16.2 425.6 %copy-start.28 = (f32[128]{0:T(128)}, f32[128]{0:T(128)S(1)}, u32[]{:S(2)}) copy-start(f32[128]{0:T(128)S(1)} %get-tuple-element.178) | copy-start | bytes 1540
  16.2 425.6 %copy-start.30 = (f32[128]{0:T(128)}, f32[128]{0:T(128)S(1)}, u32[]{:S(2)}) copy-start(f32[128]{0:T(128)S(1)} %get-tuple-element.179) | copy-start | bytes 1540
  17.2 424.7 %copy-start.32 = (f32[128]{0:T(128)}, f32[128]{0:T(128)S(1)}, u32[]{:S(2)}) copy-start(f32[128]{0:T(128)S(1)} %get-tuple-element.131) | copy-start | bytes 1540
  17.2 424.7 %copy-start.34 = (f32[128]{0:T(128)}, f32[128]{0:T(128)S(1)}, u32[]{:S(2)}) copy-start(f32[128]{0:T(128)S(1)} %get-tuple-element.132) | copy-start | bytes 1540
  17.2 424.7 %copy-start.36 = (f32[128]{0:T(128)}, f32[128]{0:T(128)S(1)}, u32[]{:S(2)}) copy-start(f32[128]{0:T(128)S(1)} %get-tuple-element.133) | copy-start | bytes 1540
  17.2 424.7 %copy-start.38 = (f32[128]{0:T(128)}, f32[128]{0:T(128)S(1)}, u32[]{:S(2)}) copy-start(f32[128]{0:T(128)S(1)} %get-tuple-element.134) | copy-start | bytes 1540
  17.2 424.7 %copy-start.40 = (f32[128]{0:T(128)}, f32[128]{0:T(128)S(1)}, u32[]{:S(2)}) copy-start(f32[128]{0:T(128)S(1)} %get-tuple-element.135) | copy-start | bytes 1540
  17.2 424.7 %copy-start.42 = (f32[128]{0:T(128)}, f32[128]{0:T(128)S(1)}, u32[]{:S(2)}) copy-start(f32[128]{0:T(128)S(1)} %get-tuple-element.136) | copy-start | bytes 1540
  17.3 424.7 %copy-start.44 = (f32[128]{0:T(128)}, f32[128]{0:T(128)S(1)}, u32[]{:S(2)}) copy-start(f32[128]{0:T(128)S(1)} %get-tuple-element.137) | copy-start | bytes 1540
  17.3 424.7 %copy-start.46 = (f32[128]{0:T(128)}, f32[128]{0:T(128)S(1)}, u32[]{:S(2)}) copy-start(f32[128]{0:T(128)S(1)} %get-tuple-element.138) | copy-start | bytes 1540
  17.3 424.7 %copy-start.48 = (f32[128]{0:T(128)}, f32[128]{0:T(128)S(1)}, u32[]{:S(2)}) copy-start(f32[128]{0:T(128)S(1)} %get-tuple-element.139) | copy-start | bytes 1540
  17.3 424.7 %copy-start.50 = (f32[128]{0:T(128)}, f32[128]{0:T(128)S(1)}, u32[]{:S(2)}) copy-start(f32[128]{0:T(128)S(1)} %get-tuple-element.140) | copy-start | bytes 1540
  17.3 424.7 %copy-start.52 = (f32[128]{0:T(128)}, f32[128]{0:T(128)S(1)}, u32[]{:S(2)}) copy-start(f32[128]{0:T(128)S(1)} %get-tuple-element.141) | copy-start | bytes 1540
  17.3 424.7 %copy-start.54 = (f32[128]{0:T(128)}, f32[128]{0:T(128)S(1)}, u32[]{:S(2)}) copy-start(f32[128]{0:T(128)S(1)} %get-tuple-element.142) | copy-start | bytes 1540
  17.3 424.7 %copy-start.56 = (f32[128]{0:T(128)}, f32[128]{0:T(128)S(1)}, u32[]{:S(2)}) copy-start(f32[128]{0:T(128)S(1)} %get-tuple-element.143) | copy-start | bytes 1540
  17.3 424.7 %copy-start.58 = (f32[128]{0:T(128)}, f32[128]{0:T(128)S(1)}, u32[]{:S(2)}) copy-start(f32[128]{0:T(128)S(1)} %get-tuple-element.144) | copy-start | bytes 1540
  17.3 424.7 %copy-start.60 = (f32[128]{0:T(128)}, f32[128]{0:T(128)S(1)}, u32[]{:S(2)}) copy-start(f32[128]{0:T(128)S(1)} %get-tuple-element.145) | copy-start | bytes 1540
  17.3 424.7 %copy-start.62 = (f32[128]{0:T(128)}, f32[128]{0:T(128)S(1)}, u32[]{:S(2)}) copy-start(f32[128]{0:T(128)S(1)} %get-tuple-element.146) | copy-start | bytes 1540
  17.4 424.7 %copy-start.64 = (f32[128]{0:T(128)}, f32[128]{0:T(128)S(1)}, u32[]{:S(2)}) copy-start(f32[128]{0:T(128)S(1)} %get-tuple-element.147) | copy-start | bytes 1540
  17.4 424.7 %copy-start.66 = (f32[128]{0:T(128)}, f32[128]{0:T(128)S(1)}, u32[]{:S(2)}) copy-start(f32[128]{0:T(128)S(1)} %get-tuple-element.148) | copy-start | bytes 1540
  17.4 424.7 %copy-start.68 = (f32[128]{0:T(128)}, f32[128]{0:T(128)S(1)}, u32[]{:S(2)}) copy-start(f32[128]{0:T(128)S(1)} %get-tuple-element.149) | copy-start | bytes 1540
  19.0 423.1 %copy-start.70 = (f32[128]{0:T(128)}, f32[128]{0:T(128)S(1)}, u32[]{:S(2)}) copy-start(f32[128]{0:T(128)S(1)} %get-tuple-element.150) | copy-start | bytes 1540
  19.0 423.1 %copy-start.72 = (f32[128]{0:T(128)}, f32[128]{0:T(128)S(1)}, u32[]{:S(2)}) copy-start(f32[128]{0:T(128)S(1)} %get-tuple-element.151) | copy-start | bytes 1540
  19.0 423.1 %copy-start.74 = (f32[128]{0:T(128)}, f32[128]{0:T(128)S(1)}, u32[]{:S(2)}) copy-start(f32[128]{0:T(128)S(1)} %get-tuple-element.152) | copy-start | bytes 1540
  19.0 423.1 %copy-start.76 = (f32[128]{0:T(128)}, f32[128]{0:T(128)S(1)}, u32[]{:S(2)}) copy-start(f32[128]{0:T(128)S(1)} %get-tuple-element.153) | copy-start | bytes 1540
  19.0 423.1 %copy-start.78 = (f32[128]{0:T(128)}, f32[128]{0:T(128)S(1)}, u32[]{:S(2)}) copy-start(f32[128]{0:T(128)S(1)} %get-tuple-element.154) | copy-start | bytes 1540
  19.0 423.1 %copy-start.80 = (f32[128]{0:T(128)}, f32[128]{0:T(128)S(1)}, u32[]{:S(2)}) copy-start(f32[128]{0:T(128)S(1)} %get-tuple-element.155) | copy-start | bytes 1540
  19.0 423.1 %copy-start.82 = (f32[128]{0:T(128)}, f32[128]{0:T(128)S(1)}, u32[]{:S(2)}) copy-start(f32[128]{0:T(128)S(1)} %get-tuple-element.156) | copy-start | bytes 1540
  19.0 423.1 %copy-start.84 = (f32[128]{0:T(128)}, f32[128]{0:T(128)S(1)}, u32[]{:S(2)}) copy-start(f32[128]{0:T(128)S(1)} %get-tuple-element.157) | copy-start | bytes 1540
  19.1 423.1 %copy-start.86 = (f32[128]{0:T(128)}, f32[128]{0:T(128)S(1)}, u32[]{:S(2)}) copy-start(f32[128]{0:T(128)S(1)} %get-tuple-element.158) | copy-start | bytes 1540
  19.1 423.1 %copy-start.88 = (f32[128]{0:T(128)}, f32[128]{0:T(128)S(1)}, u32[]{:S(2)}) copy-start(f32[128]{0:T(128)S(1)} %get-tuple-element.159) | copy-start | bytes 1540
  19.1 423.1 %copy-start.90 = (f32[128]{0:T(128)}, f32[128]{0:T(128)S(1)}, u32[]{:S(2)}) copy-start(f32[128]{0:T(128)S(1)} %get-tuple-element.160) | copy-start | bytes 1540
  19.1 423.1 %copy-start.91 = (f32[128]{0:T(128)}, f32[128]{0:T(128)S(1)}, u32[]{:S(2)}) copy-start(f32[128]{0:T(128)S(1)} %get-tuple-element.161) | copy-start | bytes 1540
  384.8 18.4 %slice-start.3 = ((s8[12582912]{0:T(1024)(128)(4,1)}), s8[4194304]{0:T(1024)(128)(4,1)S(1)}, s32[]{:S(2)}) async-start(s8[12582912]{0:T(1024)(128)(4,1)} %bitcast.264), calls=%async_computation.6 | async-start | bytes 8388608
  387.6 15.6 %slice-start.4 = ((s8[12582912]{0:T(1024)(128)(4,1)}), s8[4194304]{0:T(1024)(128)(4,1)S(1)}, s32[]{:S(2)}) async-start(s8[12582912]{0:T(1024)(128)(4,1)} %bitcast.264), calls=%async_computation.7 | async-start | bytes 8388608
  387.6 15.6 %slice-start.5 = ((s8[12582912]{0:T(1024)(128)(4,1)}), s8[4194304]{0:T(1024)(128)(4,1)S(1)}, s32[]{:S(2)}) async-start(s8[12582912]{0:T(1024)(128)(4,1)} %bitcast.264), calls=%async_computation.8 | async-start | bytes 8388608
  437.1 5.1 copy-start.105
  496.7 623.7 %all-gather.7.cloned.1.call-start = ((), (), s32[]{:S(2)}) async-start(), calls=%async_computation.1 | async-start | bytes 12779520 | tf_op jit(solution)/shard_map/all_gather | solution.py:161
  508.2 5.9 copy-start.92
  508.2 5.9 copy-start.93
  508.2 5.9 copy-start.94
  508.2 5.9 copy-start.95
  508.2 5.9 copy-start.96
  508.2 5.9 copy-start.97
  508.2 5.9 copy-start.98
  508.2 5.9 copy-start.99
  508.2 5.9 copy-start.100
  508.2 10.2 copy-start.4
  518.4 4.1 copy-start.101
  518.4 4.1 copy-start.102
  518.4 4.1 copy-start.103
  1120.4 18.4 %slice-start = ((s8[12582912]{0:T(1024)(128)(4,1)}), s8[4194304]{0:T(1024)(128)(4,1)S(1)}, s32[]{:S(2)}) async-start(s8[12582912]{0:T(1024)(128)(4,1)} %bitcast.258), calls=%async_computation.3 | async-start | bytes 8388608
  1123.1 15.6 %slice-start.1 = ((s8[12582912]{0:T(1024)(128)(4,1)}), s8[4194304]{0:T(1024)(128)(4,1)S(1)}, s32[]{:S(2)}) async-start(s8[12582912]{0:T(1024)(128)(4,1)} %bitcast.258), calls=%async_computation.4 | async-start | bytes 8388608
  1123.2 15.6 %slice-start.2 = ((s8[12582912]{0:T(1024)(128)(4,1)}), s8[4194304]{0:T(1024)(128)(4,1)S(1)}, s32[]{:S(2)}) async-start(s8[12582912]{0:T(1024)(128)(4,1)} %bitcast.258), calls=%async_computation.5 | async-start | bytes 8388608
  1175.2 16.4 %copy-start.1 = (bf16[128,512]{1,0:T(8,128)(2,1)S(1)}, bf16[128,512]{1,0:T(8,128)(2,1)}, u32[]{:S(2)}) copy-start(bf16[128,512]{1,0:T(8,128)(2,1)} %param.19) | copy-start | bytes 393220
  (56 other events, 94.2 us)
Sparse Core Ops, SparseCore 0:
  10.4 374.3 all-gather.4
  496.8 251.4 all-reduce.7
  750.1 370.2 all-gather.6
where the time goes:
time: 1200 us
  waiting for transfers between devices  880 us (73%)
  other arithmetic  91 us (8%)
  blocking collectives  76 us (6%)
  matrix products  71.1 us (6%)
  local copies, waits for them, and re-layouts  61.8 us (5%)
  between operations  17.8 us (1%)
    all_gather x2, waiting for transfers between devices, by_frames(): gathered = collect(lax.all_gather(frame, 'tiles', axis=0, tiled=True))  734 us
    psum x1, waiting for transfers between devices, on_device(): lax.psum((grad_parts[0], grad_parts[1], grad_parts[2], grad_parts[3], gra...  146 us
    psum x1, blocking collectives, on_device(): lax.psum((grad_parts[0], grad_parts[1], grad_parts[2], grad_parts[3], gra...  76 us
    dot_general x2, matrix products, collect(): jnp.einsum('jn,njsrtc->jsrtc', chosen, expand(incoming), preferred_elemen...  49.1 us
    unnamed x242, local copies, waits for them, and re-layouts  40.7 us
  transfers between devices with their start and end apart: 3, of which 3 were waited for; matrix products, arithmetic and copies ran while one was open for 3% of the time, Pallas kernels for 0%

commit v1 on v0

v1 whole, which is shorter than its diff:
```python
import functools
import math

import jax
import jax.numpy as jnp
from jax import lax
from jax.experimental import pallas as pl
from jax.experimental.pallas import tpu as pltpu
from jax.sharding import PartitionSpec as P

MESH = pl.DeviceIdType.MESH
F32 = jnp.float32
BF16 = jnp.bfloat16

T = 64
C = 128
HID = 512
NT = 64
PW = T + 6
NCH = 52
ROWS = 4
CELLS = ROWS * T
STEPS = T // ROWS
VMEM_LIMIT = 56 * 1024 * 1024

SUM_ROWS = 1040
TAP_ROWS = 56
ALL_ROWS = 1280
HALF = ALL_ROWS // 2
PIECE = HALF // 16
SCALE = 1.0 / math.sqrt(4 * NT * T * T)


def pack_natural(x_ref, frame, left, right, corner):
    for m in range(3):
        for a in range(4):
            frame[4 * m + a] = x_ref[T - 3 + m, pl.ds(16 * a, 16), :]
            frame[12 + 4 * m + a] = x_ref[m, pl.ds(16 * a, 16), :]
    left[...] = x_ref[:, 0:16, :].astype(F32).reshape(T * 16, C)
    right[...] = x_ref[:, T - 16 : T, :].astype(F32).reshape(T * 16, C)
    for c in range(3):
        for b in range(4):
            frame[24 + 4 * c + b] = right[pl.ds(256 * b + 13 + c, 16, stride=16), :].astype(BF16)
            frame[36 + 4 * c + b] = left[pl.ds(256 * b + c, 16, stride=16), :].astype(BF16)
    for n, (rows, cols, at) in enumerate(
        ((T - 3, right, 13), (T - 3, left, 0), (0, right, 13), (0, left, 0))
    ):
        corner[...] = jnp.zeros((16, C), F32)
        for r in range(3):
            corner[pl.ds(4 * r, 3), :] = cols[pl.ds((rows + r) * 16 + at, 3), :]
        frame[48 + n] = corner[...].astype(BF16)


def pack_dealt(g_ref, frame, left, right, corner):
    for m in range(3):
        for a in range(4):
            frame[4 * m + a] = g_ref[T - 3 + m, pl.ds(16 * a, 16), :]
            frame[12 + 4 * m + a] = g_ref[m, pl.ds(16 * a, 16), :]
    left[...] = g_ref[:, 0:32, :].astype(F32).reshape(T * 32, C)
    right[...] = g_ref[:, T - 32 : T, :].astype(F32).reshape(T * 32, C)
    for c in range(3):
        for b in range(4):
            frame[24 + 4 * c + b] = right[pl.ds(512 * b + 8 * c + 15, 16, stride=32), :].astype(BF16)
            frame[36 + 4 * c + b] = left[pl.ds(512 * b + 8 * c, 16, stride=32), :].astype(BF16)
    for n, (rows, cols, at) in enumerate(
        ((T - 3, right, 15), (T - 3, left, 0), (0, right, 15), (0, left, 0))
    ):
        corner[...] = jnp.zeros((16, C), F32)
        for r in range(3):
            for c in range(3):
                corner[pl.ds(4 * r + c, 1), :] = cols[pl.ds((rows + r) * 32 + at + 8 * c, 1), :]
        frame[48 + n] = corner[...].astype(BF16)


def wait_bytes(ref, count, sem):
    part = ref.at[pl.ds(0, count)]
    pltpu.make_async_copy(part, part, sem).wait()


def exchange_kernel(
    pack, src_ref, x_ref, halo_ref, frame, left, right, corner, held, chosen, send1, recv1, send2, recv2
):
    me = lax.axis_index("tiles")
    barrier = pltpu.get_barrier_semaphore()

    def greet(o, carry):
        pl.semaphore_signal(
            barrier, inc=1, device_id={"tiles": lax.rem(me + o, NT)}, device_id_type=MESH
        )
        return carry

    lax.fori_loop(1, NT, greet, 0)
    pack(x_ref, frame, left, right, corner)
    held[NT] = jnp.zeros((16, C), BF16)
    pl.semaphore_wait(barrier, NT - 1)

    def spread(o, carry):
        chunk = lax.rem(me + o, NT)

        @pl.when(chunk < NCH)
        def _():
            pltpu.make_async_remote_copy(
                src_ref=frame.at[chunk],
                dst_ref=held.at[me],
                send_sem=send1,
                recv_sem=recv1,
                device_id={"tiles": chunk},
                device_id_type=MESH,
            ).start()

        return carry

    lax.fori_loop(1, NT, spread, 0)

    @pl.when(me < NCH)
    def _():
        held[me] = frame[me]
        wait_bytes(held, NT - 1, recv1)

        def hand_on(o, carry):
            to = lax.rem(me + o, NT)
            chosen[to] = held[src_ref[to]]
            pltpu.make_async_remote_copy(
                src_ref=chosen.at[to],
                dst_ref=halo_ref.at[me],
                send_sem=send2,
                recv_sem=recv2,
                device_id={"tiles": to},
                device_id_type=MESH,
            ).start()
            return carry

        lax.fori_loop(1, NT, hand_on, 0)
        halo_ref[me] = held[src_ref[me]]
        wait_bytes(halo_ref, NCH - 1, recv2)
        wait_bytes(held, NCH - 1, send1)
        wait_bytes(held, NT - 1, send2)

    @pl.when(me >= NCH)
    def _():
        wait_bytes(halo_ref, NCH, recv2)
        wait_bytes(held, NCH, send1)


def exchange(x, src, dealt, collective_id):
    width = 32 if dealt else 16
    return pl.pallas_call(
        functools.partial(exchange_kernel, pack_dealt if dealt else pack_natural),
        out_shape=jax.ShapeDtypeStruct((NCH, 16, C), BF16),
        in_specs=[
            pl.BlockSpec(memory_space=pltpu.SMEM),
            pl.BlockSpec(memory_space=pltpu.VMEM),
        ],
        out_specs=pl.BlockSpec(memory_space=pltpu.VMEM),
        scratch_shapes=[
            pltpu.VMEM((NCH, 16, C), BF16),
            pltpu.VMEM((T * width, C), F32),
            pltpu.VMEM((T * width, C), F32),
            pltpu.VMEM((16, C), F32),
            pltpu.VMEM((NT + 1, 16, C), BF16),
            pltpu.VMEM((NT, 16, C), BF16),
            pltpu.SemaphoreType.DMA,
            pltpu.SemaphoreType.DMA,
            pltpu.SemaphoreType.DMA,
            pltpu.SemaphoreType.DMA,
        ],
        compiler_params=pltpu.CompilerParams(
            collective_id=collective_id, has_side_effects=True, vmem_limit_bytes=VMEM_LIMIT
        ),
        name="exchange_grad" if dealt else "exchange_input",
    )(src, x)


PITCH = 80
QROW = 14 * 8


def build_input(sea_ref, halo_ref, nat, corner, q_ref):
    def own(p, carry):
        at = pl.multiple_of((p + 3) * PITCH + 8, 8)
        nat[pl.ds(at, T), :] = sea_ref[p].astype(F32)
        return carry

    lax.fori_loop(0, T, own, 0)
    for m in range(3):
        for a in range(4):
            nat[pl.ds(m * PITCH + 8 + 16 * a, 16), :] = halo_ref[4 * m + a].astype(F32)
            nat[pl.ds((67 + m) * PITCH + 8 + 16 * a, 16), :] = halo_ref[12 + 4 * m + a].astype(F32)
    for c in range(3):
        for b in range(4):
            at = (3 + 16 * b) * PITCH
            nat[pl.ds(at + 5 + c, 16, stride=PITCH), :] = halo_ref[24 + 4 * c + b].astype(F32)
            nat[pl.ds(at + 72 + c, 16, stride=PITCH), :] = halo_ref[36 + 4 * c + b].astype(F32)
    for n, (row, at) in enumerate(((0, 5), (0, 72), (67, 5), (67, 72))):
        corner[...] = halo_ref[48 + n].astype(F32)
        for r in range(3):
            nat[pl.ds((row + r) * PITCH + at, 3), :] = corner[pl.ds(4 * r, 3), :]

    def deal(p, carry):
        for k in range(14):
            q_ref[p, pl.ds(8 * k, 8), :] = nat[pl.ds(p * PITCH + 5 + k, 8, stride=8), :]
        return carry

    lax.fori_loop(0, PW, deal, 0)


def conv_row(q_ref, taps, row, flipped):
    acc = None
    for i in range(7):
        x = q_ref[row + i].reshape(14, 8, C)
        for j in range(7):
            tap = taps[48 - 7 * i - j] if flipped else taps[7 * i + j]
            term = x[j : j + 8] * tap
            acc = term if acc is None else acc + term
    return acc


def spread_taps(k_ref, taps):
    for i in range(7):
        for j in range(7):
            taps[7 * i + j] = jnp.broadcast_to(k_ref[i, pl.ds(j, 1), :], (8, C))


def fold(x):
    return jnp.sum(x.reshape(x.shape[0] // 8, 8, x.shape[1]), 0)


def dot(a, b, contract):
    return lax.dot_general(a, b, (contract, ((), ())), preferred_element_type=F32)


def block_kernel(
    sea_ref,
    halo_ref,
    cot_ref,
    k_ref,
    cb_ref,
    gain_ref,
    lnb_ref,
    win_ref,
    bin_ref,
    wout_ref,
    bout_ref,
    ls_ref,
    out_ref,
    g_ref,
    q_ref,
    sums_ref,
    nat,
    corner,
    taps,
    conv,
    work,
    acc_win,
    acc_wout,
    acc_bin,
    acc_vec,
):
    step = pl.program_id(0)

    @pl.when(step == 0)
    def _():
        build_input(sea_ref, halo_ref, nat, corner, q_ref)
        spread_taps(k_ref, taps)
        acc_win[...] = jnp.zeros_like(acc_win)
        acc_wout[...] = jnp.zeros_like(acc_wout)
        acc_bin[...] = jnp.zeros_like(acc_bin)
        acc_vec[...] = jnp.zeros_like(acc_vec)

    first = step * ROWS

    def one_row(p, carry):
        conv[pl.ds(pl.multiple_of(p * T, T), T), :] = conv_row(q_ref, taps, first + p, False).reshape(T, C)
        return carry

    lax.fori_loop(0, ROWS, one_row, 0)

    work[...] = cot_ref[...].astype(F32).reshape(CELLS, C)
    up = jnp.concatenate(
        [work[pl.ds(p * T + k, 8, stride=8), :] for p in range(ROWS) for k in range(8)], 0
    )
    convolved = conv[...] + cb_ref[...]
    centred = convolved - jnp.mean(convolved, -1, keepdims=True)
    inv_std = lax.rsqrt(jnp.mean(centred * centred, -1, keepdims=True) + 1e-06)
    whitened = centred * inv_std
    normed = (whitened * gain_ref[...] + lnb_ref[...]).astype(BF16)
    grad_out = up * ls_ref[...]
    grad_out16 = grad_out.astype(BF16)

    branch = bout_ref[...]
    grad_normed = None
    width = 256
    c0 = math.sqrt(2 / math.pi)
    c1 = c0 * 0.044715
    for h in range(HID // width):
        hid = pl.ds(h * width, width)
        v = dot(normed, win_ref[:, hid], ((1,), (0,))) + bin_ref[:, hid]
        v2 = v * v
        t = jnp.tanh(v * (c0 + c1 * v2))
        half = 0.5 + 0.5 * t
        act = v * half
        slope = half + act * (1.0 - t) * (c0 + (3 * c1) * v2)
        act16 = act.astype(BF16)
        branch = branch + dot(act16, wout_ref[hid, :], ((1,), (0,)))
        acc_wout[:, hid] += dot(grad_out16, act16, ((0,), (0,)))
        grad_pre = slope * dot(grad_out16, wout_ref[hid, :], ((1,), (1,)))
        grad_pre16 = grad_pre.astype(BF16)
        acc_bin[:, hid] += fold(grad_pre)
        acc_win[:, hid] += dot(normed, grad_pre16, ((0,), (0,)))
        part = dot(grad_pre16, win_ref[:, hid], ((1,), (1,)))
        grad_normed = part if grad_normed is None else grad_normed + part

    grad_white = grad_normed * gain_ref[...]
    grad_conv = inv_std * (
        grad_white
        - jnp.mean(grad_white, -1, keepdims=True)
        - whitened * jnp.mean(grad_white * whitened, -1, keepdims=True)
    )
    g_ref[...] = grad_conv.astype(BF16).reshape(ROWS, T, C)
    acc_vec[0] += fold(grad_conv)
    acc_vec[1] += fold(grad_normed * whitened)
    acc_vec[2] += fold(grad_normed)
    acc_vec[3] += fold(grad_out)
    acc_vec[4] += fold(up * branch)

    scaled = branch * ls_ref[...]
    for p in range(ROWS):
        for k in range(8):
            at = p * T + 8 * k
            work[pl.ds(p * T + k, 8, stride=8), :] = scaled[at : at + 8]
    own = sea_ref[pl.ds(first, ROWS)].astype(F32)
    out_ref[...] = (own + work[...].reshape(ROWS, T, C)).astype(BF16)

    @pl.when(step == STEPS - 1)
    def _():
        for n in range(4):
            block = pl.ds(n * C, C)
            sums_ref[block, :] = acc_win[:, block]
            sums_ref[pl.ds(512 + n * C, C), :] = acc_wout[:, block].T
            sums_ref[pl.ds(1024 + n, 1), :] = jnp.sum(acc_bin[:, block], 0, keepdims=True)
        for n in range(5):
            sums_ref[pl.ds(1028 + n, 1), :] = jnp.sum(acc_vec[n], 0, keepdims=True)
        sums_ref[pl.ds(1033, SUM_ROWS - 1033), :] = jnp.zeros((SUM_ROWS - 1033, C), F32)


def whole(shape):
    return pl.BlockSpec(shape, lambda s: (0,) * len(shape))


def block(sea, halo, cot, kernel, conv_bias, ln_gain, ln_bias, w_in, b_in, w_out, b_out, layer_scale):
    rows = pl.BlockSpec((ROWS, T, C), lambda s: (s, 0, 0))
    return pl.pallas_call(
        block_kernel,
        grid=(STEPS,),
        out_shape=(
            jax.ShapeDtypeStruct((T, T, C), BF16),
            jax.ShapeDtypeStruct((T, T, C), BF16),
            jax.ShapeDtypeStruct((PW, QROW, C), F32),
            jax.ShapeDtypeStruct((SUM_ROWS, C), F32),
        ),
        in_specs=[
            whole((T, T, C)),
            whole((NCH, 16, C)),
            rows,
            whole((7, 7, C)),
            whole((1, C)),
            whole((1, C)),
            whole((1, C)),
            whole((C, HID)),
            whole((1, HID)),
            whole((HID, C)),
            whole((1, C)),
            whole((1, C)),
        ],
        out_specs=(rows, rows, whole((PW, QROW, C)), whole((SUM_ROWS, C))),
        scratch_shapes=[
            pltpu.VMEM((PW * PITCH, C), F32),
            pltpu.VMEM((16, C), F32),
            pltpu.VMEM((49, 8, C), F32),
            pltpu.VMEM((CELLS, C), F32),
            pltpu.VMEM((CELLS, C), F32),
            pltpu.VMEM((C, HID), F32),
            pltpu.VMEM((C, HID), F32),
            pltpu.VMEM((8, HID), F32),
            pltpu.VMEM((5, 8, C), F32),
        ],
        compiler_params=pltpu.CompilerParams(
            dimension_semantics=("arbitrary",), vmem_limit_bytes=VMEM_LIMIT
        ),
        name="block",
    )(
        sea,
        halo,
        cot,
        kernel,
        conv_bias.reshape(1, C),
        ln_gain.reshape(1, C),
        ln_bias.reshape(1, C),
        w_in,
        b_in.reshape(1, HID),
        w_out,
        b_out.reshape(1, C),
        layer_scale.reshape(1, C),
    )


def build_grad(g_ref, halo_ref, corner, qg):
    lane = lax.broadcasted_iota(jnp.int32, (8, C), 0)

    def put(row, g):
        qg[row, pl.ds(24, T), :] = g.reshape(T, C)
        for k in range(3):
            qg[row, pl.ds(8 * k, 8), :] = pltpu.roll(g[5 + k], 1, 0)
            qg[row, pl.ds(88 + 8 * k, 8), :] = pltpu.roll(g[k], 7, 0)

    def own(p, carry):
        put(p + 3, g_ref[p].astype(F32).reshape(8, 8, C))
        return carry

    lax.fori_loop(0, T, own, 0)
    for m in range(3):
        for row, base in ((m, 0), (67 + m, 12)):
            put(
                row,
                jnp.concatenate(
                    [halo_ref[base + 4 * m + a].astype(F32).reshape(2, 8, C) for a in range(4)], 0
                ),
            )
    for c in range(3):
        for b in range(4):
            corner[...] = halo_ref[24 + 4 * c + b].astype(F32)
            for r in range(16):
                qg[3 + 16 * b + r, pl.ds(8 * c, 1), :] = corner[pl.ds(r, 1), :]
            corner[...] = halo_ref[36 + 4 * c + b].astype(F32)
            for r in range(16):
                qg[3 + 16 * b + r, pl.ds(88 + 8 * c + 7, 1), :] = corner[pl.ds(r, 1), :]
    for n, (row, at) in enumerate(((0, 0), (0, 95), (67, 0), (67, 95))):
        corner[...] = halo_ref[48 + n].astype(F32)
        for r in range(3):
            for c in range(3):
                qg[row + r, pl.ds(at + 8 * c, 1), :] = corner[pl.ds(4 * r + c, 1), :]


def taps_kernel(g_ref, halo_ref, q_ref, cot_ref, k_ref, out_ref, tapsum_ref, corner, taps, qg, work, acc):
    step = pl.program_id(0)

    @pl.when(step == 0)
    def _():
        build_grad(g_ref, halo_ref, corner, qg)
        spread_taps(k_ref, taps)
        acc[...] = jnp.zeros_like(acc)

    first = step * ROWS

    def one_row(p, carry):
        row = first + p
        total = conv_row(qg, taps, row, True)
        at = p * T
        for k in range(8):
            work[pl.ds(at + k, 8, stride=8), :] = total[k]
        g = qg[row + 3, pl.ds(24, T), :].reshape(8, 8, C)
        for i in range(7):
            x = q_ref[row + i].reshape(14, 8, C)
            for j in range(7):
                acc[7 * i + j] += jnp.sum(x[j : j + 8] * g, 0)
        return carry

    lax.fori_loop(0, ROWS, one_row, 0)
    out_ref[...] = (cot_ref[...].astype(F32) + work[...].reshape(ROWS, T, C)).astype(BF16)

    @pl.when(step == STEPS - 1)
    def _():
        for n in range(49):
            tapsum_ref[pl.ds(n, 1), :] = jnp.sum(acc[n], 0, keepdims=True)
        tapsum_ref[pl.ds(49, TAP_ROWS - 49), :] = jnp.zeros((TAP_ROWS - 49, C), F32)


def tap_pass(g, halo, q, cot, kernel):
    rows = pl.BlockSpec((ROWS, T, C), lambda s: (s, 0, 0))
    return pl.pallas_call(
        taps_kernel,
        grid=(STEPS,),
        out_shape=(
            jax.ShapeDtypeStruct((T, T, C), BF16),
            jax.ShapeDtypeStruct((TAP_ROWS, C), F32),
        ),
        in_specs=[
            whole((T, T, C)),
            whole((NCH, 16, C)),
            whole((PW, QROW, C)),
            rows,
            whole((7, 7, C)),
        ],
        out_specs=(rows, whole((TAP_ROWS, C))),
        scratch_shapes=[
            pltpu.VMEM((16, C), F32),
            pltpu.VMEM((49, 8, C), F32),
            pltpu.VMEM((PW, QROW, C), F32),
            pltpu.VMEM((CELLS, C), F32),
            pltpu.VMEM((49, 8, C), F32),
        ],
        compiler_params=pltpu.CompilerParams(
            dimension_semantics=("arbitrary",), vmem_limit_bytes=VMEM_LIMIT
        ),
        name="taps",
    )(g, halo, q, cot, kernel)


def sum_kernel(
    sums_ref,
    tapsum_ref,
    total_ref,
    buf,
    other,
    pieces,
    part,
    line,
    sent,
    landed,
):
    t, d = lax.axis_index("tiles"), lax.axis_index("dp")
    x, zl, y = lax.div(t, 16), lax.rem(lax.div(t, 4), 4), lax.rem(t, 4)
    zh, core = lax.div(d, 2), lax.rem(d, 2)
    q, z = 4 * x + y, 4 * zh + zl

    def in_plane(o):
        there = lax.rem(q + o, 16)
        return there, {"tiles": 16 * lax.div(there, 4) + 4 * zl + lax.rem(there, 4), "dp": d}

    def in_line(o):
        there = lax.rem(z + o, 8)
        return {"tiles": 16 * x + 4 * lax.rem(there, 4) + y, "dp": 2 * lax.div(there, 4) + core}

    twin = {"tiles": t, "dp": 2 * zh + (1 - core)}

    def send(stage, src, dst, device):
        copy = pltpu.make_async_remote_copy(
            src_ref=src,
            dst_ref=dst,
            send_sem=sent.at[stage],
            recv_sem=landed.at[stage],
            device_id=device,
            device_id_type=MESH,
        )
        copy.start()
        return copy

    def each(count, do):
        def body(o, carry):
            do(o)
            return carry

        lax.fori_loop(1, count, body, 0)

    barrier = pltpu.get_barrier_semaphore()
    pl.semaphore_signal(barrier, inc=1, device_id=twin, device_id_type=MESH)
    each(16, lambda o: pl.semaphore_signal(barrier, inc=1, device_id=in_plane(o)[1], device_id_type=MESH))
    each(8, lambda o: pl.semaphore_signal(barrier, inc=1, device_id=in_line(o), device_id_type=MESH))
    buf[pl.ds(0, SUM_ROWS), :] = sums_ref[...]
    buf[pl.ds(SUM_ROWS, TAP_ROWS), :] = tapsum_ref[...]
    rest = SUM_ROWS + TAP_ROWS
    buf[pl.ds(rest, ALL_ROWS - rest), :] = jnp.zeros((ALL_ROWS - rest, C), F32)
    pl.semaphore_wait(barrier, 23)

    mine = pl.multiple_of(core * HALF, HALF)
    yours = pl.multiple_of((1 - core) * HALF, HALF)
    first = send(0, buf.at[pl.ds(yours, HALF), :], other, twin)
    first.wait()
    other[...] += buf[pl.ds(mine, HALF), :]

    def scatter(o):
        there, device = in_plane(o)
        at = pl.multiple_of(there * PIECE, PIECE)
        send(1, other.at[pl.ds(at, PIECE), :], pieces.at[q], device)

    each(16, scatter)
    here = pl.multiple_of(q * PIECE, PIECE)
    pieces[q] = other[pl.ds(here, PIECE), :]
    wait_bytes(pieces, 15, landed.at[1])
    part[...] = jnp.sum(pieces[...], 0)

    each(8, lambda o: send(2, part, line.at[z], in_line(o)) and None)
    line[z] = part[...]
    wait_bytes(line, 7, landed.at[2])
    mine_total = total_ref.at[pl.ds(mine, HALF), :]
    total_ref[pl.ds(pl.multiple_of(mine + here, 8), PIECE), :] = jnp.sum(line[...], 0) * SCALE

    def gather(o):
        spot = total_ref.at[pl.ds(pl.multiple_of(mine + here, 8), PIECE), :]
        send(3, spot, spot, in_plane(o)[1])

    each(16, gather)
    wait_bytes(pieces, 15, landed.at[3])
    last = send(4, mine_total, mine_total, twin)
    wait_bytes(pieces, 15, sent.at[1])
    wait_bytes(line, 7, sent.at[2])
    wait_bytes(pieces, 15, sent.at[3])
    last.wait()


def sum_all(sums, tapsum):
    return pl.pallas_call(
        sum_kernel,
        out_shape=jax.ShapeDtypeStruct((ALL_ROWS, C), F32),
        in_specs=[pl.BlockSpec(memory_space=pltpu.VMEM)] * 2,
        out_specs=pl.BlockSpec(memory_space=pltpu.VMEM),
        scratch_shapes=[
            pltpu.VMEM((ALL_ROWS, C), F32),
            pltpu.VMEM((HALF, C), F32),
            pltpu.VMEM((16, PIECE, C), F32),
            pltpu.VMEM((PIECE, C), F32),
            pltpu.VMEM((8, PIECE, C), F32),
            pltpu.SemaphoreType.DMA((5,)),
            pltpu.SemaphoreType.DMA((5,)),
        ],
        compiler_params=pltpu.CompilerParams(
            collective_id=3, has_side_effects=True, vmem_limit_bytes=VMEM_LIMIT
        ),
        name="sum_all",
    )(sums, tapsum)


def sources(tile_deal, adjacency):
    me = lax.axis_index("tiles")
    way = jnp.where(me < 48, lax.div(me, 12), lax.rem(me, 4) + 4)
    ids = jnp.arange(NT, dtype=jnp.int32)
    picked = jnp.sum(jnp.where(jnp.arange(8)[None, :] == way, adjacency, 0), 1)
    near = jnp.sum(jnp.where(tile_deal[:, None] == ids[None, :], picked[None, :], 0), 1)
    holder = jnp.sum(jnp.where(near[:, None] == tile_deal[None, :], ids[None, :], 0), 1)
    return jnp.where(near < 0, NT, holder).astype(jnp.int32)


def on_device(
    sea_state,
    cotangent,
    kernel,
    conv_bias,
    ln_gain,
    ln_bias,
    w_in,
    b_in,
    w_out,
    b_out,
    layer_scale,
    tile_deal,
    adjacency,
):
    sea, cot = sea_state[0, 0], cotangent[0, 0]
    src = sources(tile_deal, adjacency)
    halo = exchange(sea, src, False, 1)
    out, grad_conv, q, sums = block(
        sea, halo, cot, kernel, conv_bias, ln_gain, ln_bias, w_in, b_in, w_out, b_out, layer_scale
    )
    grad_halo = exchange(grad_conv, src, True, 2)
    grad_field, tapsum = tap_pass(grad_conv, grad_halo, q, cot, kernel)
    total = sum_all(sums, tapsum)
    return (
        out[None, None],
        grad_field[None, None],
        total[SUM_ROWS : SUM_ROWS + 49].reshape(7, 7, C),
        total[1028],
        total[1029],
        total[1030],
        total[:512].reshape(4, C, C).transpose(1, 0, 2).reshape(C, HID),
        total[1024:1028].reshape(HID),
        total[512:1024],
        total[1031],
        total[1032],
    )


def solution(mesh):
    field = P("dp", "tiles", None, None, None)
    return jax.shard_map(
        on_device,
        mesh=mesh,
        in_specs=(field, field) + (P(),) * 11,
        out_specs=(field, field) + (P(),) * 9,
        check_vma=False,
    )
```

time: 1200 us -> 151 us (0.13)
  the two profiles are of different devices: /device:TPU:8 before, /device:TPU:1 now
where the time goes in v1:
time: 151 us
  Pallas kernels  141 us (93%)
  local copies, waits for them, and re-layouts  6.48 us (4%)
  other arithmetic  2.97 us (2%)
    pallas_call x2, Pallas kernels, exchange(): pl.pallas_call(functools.partial(exchange_kernel, pack_dealt if dealt els...  46.3 us
    pallas_call x1, Pallas kernels, block(): pl.pallas_call(block_kernel, grid=(STEPS,), out_shape=(jax.ShapeDtypeStru...  37.2 us
    pallas_call x1, Pallas kernels, sum_all(): pl.pallas_call(sum_kernel, out_shape=jax.ShapeDtypeStruct((ALL_ROWS, C),...  34.2 us
    pallas_call x1, Pallas kernels, tap_pass(): pl.pallas_call(taps_kernel, grid=(STEPS,), out_shape=(jax.ShapeDtypeStruc...  22.9 us

profile of v1, /device:TPU:1, one launch (start us, length us, event | category | flops | bytes accessed | tf_op | source)
XLA Modules:
  0.0 150.8 jit_solution(9610027177367417298)
XLA Ops:
  0.7 0.8 select_reduce_fusion.2
  1.4 0.8 select_reduce_fusion.1
  2.3 0.8 select_reduce_fusion
  3.1 0.5 compare_select_fusion.src_ref
  3.6 25.0 %exchange_input.1.halo_ref = bf16[52,16,128]{2,1,0:T(8,128)(2,1)} custom-call(s32[64]{0:T(128)} %compare_select_fusion.src_ref, bf16[64,64,128]{2,1,0:T(8,128)(2,1)} %bitcast.29), custom_call_target="tpu_custom_call" | custom-call | tf_op jit(solution)/shard_map/exchange_input/pallas_call | solution.py:147
  28.7 37.2 %block.1 = (bf16[64,64,128]{2,1,0:T(8,128)(2,1)}, bf16[64,64,128]{2,1,0:T(8,128)(2,1)}, f32[70,112,128]{2,1,0:T(8,128)}, f32[1040,128]{1,0:T(8,128)}) custom-call(bf16[64,64,128]{2,1,0:T(8,128)(2,1)} %bitcast.30, bf16[52,16,128]{2,1,0:T(8,128)(2,1)} %exchange_input.1.halo_ref, bf16[64,64,128]{2,1,0:T(8,128)(2,1)} %bitcast.31, f32[7,7,128]{2,1,0:T(8,128)} %k_ref.3, ...), custom_call_target="tpu_custom_call" | custom-call | tf_op jit(solution)/shard_map/block/pallas_call | solution.py:352
  65.8 21.3 %exchange_grad.1.halo_ref = bf16[52,16,128]{2,1,0:T(8,128)(2,1)} custom-call(s32[64]{0:T(128)} %compare_select_fusion.src_ref, bf16[64,64,128]{2,1,0:T(8,128)(2,1)} %get-tuple-element.18.x_ref.g_ref), custom_call_target="tpu_custom_call" | custom-call | tf_op jit(solution)/shard_map/exchange_grad/pallas_call | solution.py:147
  87.2 22.9 %taps.1 = (bf16[64,64,128]{2,1,0:T(8,128)(2,1)}, f32[56,128]{1,0:T(8,128)}) custom-call(bf16[64,64,128]{2,1,0:T(8,128)(2,1)} %get-tuple-element.18.x_ref.g_ref, bf16[52,16,128]{2,1,0:T(8,128)(2,1)} %exchange_grad.1.halo_ref, f32[70,112,128]{2,1,0:T(8,128)} %get-tuple-element.19.q_ref, bf16[64,64,128]{2,1,0:T(8,128)(2,1)} %bitcast.32, f32[7,7,128]{2,1,0:T(8,128)} %k_ref.3), custom_call_target="tpu_custom_call" | custom-call | tf_op jit(solution)/shard_map/taps/pallas_call | solution.py:480
  110.1 34.2 %sum_all.1 = f32[1280,128]{1,0:T(8,128)} custom-call(f32[1040,128]{1,0:T(8,128)} %get-tuple-element.21.sums_ref, f32[56,128]{1,0:T(8,128)} %get-tuple-element.22.tapsum_ref), custom_call_target="tpu_custom_call" | custom-call | tf_op jit(solution)/shard_map/sum_all/pallas_call | solution.py:602
  144.3 1.3 slice_bitcast_fusion
  145.6 1.4 slice_bitcast_fusion.1
  146.9 0.8 slice.27
  147.7 1.8 %fusion = (f32[512,128]{1,0:T(8,128)}, f32[512,128]{1,0:T(8,128)S(1)}) fusion(f32[1280,128]{1,0:T(8,128)} %sum_all.1), kind=kLoop, calls=%fused_computation.13 | loop fusion | bytes 1048576 | tf_op jit(solution)/shard_map/slice | solution.py:666
  149.5 0.7 copy.28
  150.2 0.6 reshape.67
  (1 shorter events, 0.0 us)

commit v2 on v0

v2 whole, which is shorter than its diff:
```python
import functools
import math

import jax
import jax.numpy as jnp
from jax import lax
from jax.experimental import pallas as pl
from jax.experimental.pallas import tpu as pltpu
from jax.sharding import PartitionSpec as P

MESH = pl.DeviceIdType.MESH
F32 = jnp.float32
BF16 = jnp.bfloat16

T = 64
C = 128
HID = 512
NT = 64
PW = T + 6
NCH = 52
VMEM_LIMIT = 60 * 1024 * 1024

QROW = 14 * 8
WPOS = (6, 4, 2, 0, 1, 3, 5, 7)
WOF = tuple(WPOS.index(n) for n in range(8))
BLOCKS = (
    ((1, 7), (9, 15)),
    ((0, 1), (7, 9), (15, 24)),
    ((24, 36),),
    ((36, 48),),
    ((48, 64),),
)

ALL_ROWS = 1024
HALF = ALL_ROWS // 2
PIECE = HALF // 16
SMALL = 64
SCALE = 1.0 / math.sqrt(4 * NT * T * T)


def rows(start, size, stride=None):
    return pl.ds(start, size) if stride is None else pl.ds(start, size, stride=stride)


def aligned(at):
    return at if isinstance(at, int) else pl.multiple_of(at, 8)


def wait_bytes(ref, count, sem):
    part = ref.at[pl.ds(0, count)]
    pltpu.make_async_copy(part, part, sem).wait()


def loop(first, last, do):
    def body(n, carry):
        do(n)
        return carry

    lax.fori_loop(first, last, body, 0)


def margins(q, row):
    base = row * QROW
    lane = lax.rem(lax.broadcasted_iota(jnp.int32, (24, C), 0), 8)
    west = q[rows(base + 24 + 39, 24), :]
    q[rows(aligned(base), 24), :] = jnp.where(lane == 0, 0.0, west)
    east = q[rows(base + 25, 24), :]
    q[rows(aligned(base + 88), 24), :] = jnp.where(lane == 7, 0.0, east)


def pack(q, frame, corner):
    for m in range(3):
        for a in range(4):
            frame[4 * m + a] = q[rows((T + m) * QROW + 24 + 16 * a, 16), :].astype(BF16)
            frame[12 + 4 * m + a] = q[rows((3 + m) * QROW + 24 + 16 * a, 16), :].astype(BF16)
    for c in range(3):
        for b in range(4):
            base = (3 + 16 * b) * QROW + 24
            frame[24 + 4 * c + b] = q[rows(base + 8 * (5 + c) + 7, 16, QROW), :].astype(BF16)
            frame[36 + 4 * c + b] = q[rows(base + 8 * c, 16, QROW), :].astype(BF16)
    corner[...] = jnp.zeros((16, C), F32)
    for n, (row, at) in enumerate(((T, 47), (T, 0), (3, 47), (3, 0))):
        for r in range(3):
            for c in range(3):
                corner[rows(4 * r + c, 1), :] = q[rows((row + r) * QROW + 24 + at + 8 * c, 1), :]
        frame[48 + n] = corner[...].astype(BF16)


def put_sides(q, halo):
    for c in range(3):
        for b in range(4):
            base = (3 + 16 * b) * QROW
            q[rows(base + 8 * c, 16, QROW), :] = halo[24 + 4 * c + b].astype(F32)
            q[rows(base + 88 + 8 * c + 7, 16, QROW), :] = halo[36 + 4 * c + b].astype(F32)


def put_ends(q, halo, corner):
    for m in range(3):
        for row, first in ((m, 0), (67 + m, 12)):
            for a in range(4):
                q[rows(row * QROW + 24 + 16 * a, 16), :] = halo[first + 4 * m + a].astype(F32)
            margins(q, row)
    for n, (row, at) in enumerate(((0, 0), (0, 95), (67, 0), (67, 95))):
        corner[...] = halo[48 + n].astype(F32)
        for r in range(3):
            for c in range(3):
                q[rows((row + r) * QROW + at + 8 * c, 1), :] = corner[rows(4 * r + c, 1), :]


def tap_at(taps, i, j, flipped):
    return taps[48 - 7 * i - j] if flipped else taps[7 * i + j]


def convolve(q, taps, field, group, flipped):
    first = group * 8
    for w in range(0, 8, 2):
        acc = [None] * 8
        for m in range(14):
            x = q[rows(aligned((first + m) * QROW + 8 * w), 64), :].reshape(8, 8, C)
            for r in range(8):
                i = m - r
                if 0 <= i < 7:
                    for j in range(7):
                        term = x[j : j + 2] * tap_at(taps, i, j, flipped)
                        acc[r] = term if acc[r] is None else acc[r] + term
        for r in range(8):
            for n in range(2):
                field[rows(aligned(WPOS[w + n] * 512 + 8 * (first + r)), 8), :] = acc[r][n]


def add_sides(q, taps, field, group, flipped):
    first = group * 8
    for side in range(2):
        acc = [None] * 3
        for i in range(7):
            for c in range(3):
                at = 8 * c if side == 0 else 88 + 8 * c + 7
                x = q[rows((first + i) * QROW + at, 8, QROW), :]
                for e in range(3):
                    j = c - e if side == 0 else 6 + c - e
                    if 0 <= j < 7:
                        term = x * tap_at(taps, i, j, flipped)
                        acc[e] = term if acc[e] is None else acc[e] + term
        for e in range(3):
            w, s = (e, 0) if side == 0 else (5 + e, 7)
            spot = rows(WPOS[w] * 512 + first * 8 + s, 8, 8)
            field[spot, :] = field[spot, :] + acc[e]


def add_ends(q, taps, field, flipped):
    for e in range(3):
        for row, inputs in ((e, range(3 - e)), (61 + e, range(6 - e, 7))):
            acc = None
            for i in inputs:
                x = q[rows((row + i) * QROW, QROW), :].reshape(14, 8, C)
                for j in range(7):
                    term = x[j : j + 8] * tap_at(taps, i, j, flipped)
                    acc = term if acc is None else acc + term
            for w in range(8):
                spot = rows(WPOS[w] * 512 + 8 * row, 8)
                field[spot, :] = field[spot, :] + acc[w]


def neighbours_in(q, halo, corner, taps, field, flipped):
    put_sides(q, halo)
    loop(0, 8, lambda group: add_sides(q, taps, field, group, flipped))
    put_ends(q, halo, corner)
    add_ends(q, taps, field, flipped)


def tap_sums(q, qg, acc, p):
    g = qg[rows(aligned((p + 3) * QROW + 24), T), :].reshape(8, 8, C)
    for i in range(7):
        x = q[rows(aligned((p + i) * QROW), QROW), :].reshape(14, 8, C)
        for j in range(7):
            acc[7 * i + j] += jnp.sum(x[j : j + 8] * g, 0)


def fold(x):
    return jnp.sum(x.reshape(x.shape[0] // 8, 8, x.shape[1]), 0)


def dot(a, b, contract):
    return lax.dot_general(a, b, (contract, ((), ())), preferred_element_type=F32)


def pointwise(runs, field, up_field, weights, nat, qg, sums):
    cb_ref, gain_ref, lnb_ref, win_ref, bin_ref, wout_ref, bout_ref, ls_ref = weights
    acc_win, acc_wout, acc_bin, acc_vec = sums

    def take(ref):
        parts = [ref[rows(a * 64, (b - a) * 64), :] for a, b in runs]
        return parts[0] if len(parts) == 1 else jnp.concatenate(parts, 0)

    convolved = take(field) + cb_ref[...]
    up = take(up_field)
    centred = convolved - jnp.mean(convolved, -1, keepdims=True)
    inv_std = lax.rsqrt(jnp.mean(centred * centred, -1, keepdims=True) + 1e-06)
    whitened = centred * inv_std
    normed = (whitened * gain_ref[...] + lnb_ref[...]).astype(BF16)
    grad_out = up * ls_ref[...]
    grad_out16 = grad_out.astype(BF16)
    c0 = math.sqrt(2 / math.pi)
    c1 = c0 * 0.044715
    v = dot(normed, win_ref[...], ((1,), (0,))) + bin_ref[...]
    v2 = v * v
    t = jnp.tanh(v * (c0 + c1 * v2))
    half = 0.5 + 0.5 * t
    act = v * half
    slope = half + act * (1.0 - t) * (c0 + (3 * c1) * v2)
    act16 = act.astype(BF16)
    branch = bout_ref[...] + dot(act16, wout_ref[...], ((1,), (0,)))
    acc_wout[...] += dot(grad_out16, act16, ((0,), (0,)))
    grad_pre = slope * dot(grad_out16, wout_ref[...], ((1,), (1,)))
    grad_pre16 = grad_pre.astype(BF16)
    acc_bin[...] += fold(grad_pre)
    acc_win[...] += dot(normed, grad_pre16, ((0,), (0,)))
    grad_normed = dot(grad_pre16, win_ref[...], ((1,), (1,)))
    grad_white = grad_normed * gain_ref[...]
    grad_conv = inv_std * (
        grad_white
        - jnp.mean(grad_white, -1, keepdims=True)
        - whitened * jnp.mean(grad_white * whitened, -1, keepdims=True)
    )
    acc_vec[0] += fold(grad_conv)
    acc_vec[1] += fold(grad_normed * whitened)
    acc_vec[2] += fold(grad_normed)
    acc_vec[3] += fold(grad_out)
    acc_vec[4] += fold(up * branch)
    scaled = branch * ls_ref[...]
    rounded = grad_conv.astype(BF16).astype(F32)
    at = 0
    for a, b in runs:
        for n in range(8 * a, 8 * b):
            w, p = WOF[n // 64], n % 64
            nat[rows(p * T + w, 8, 8), :] = scaled[at : at + 8]
            qg[rows((p + 3) * QROW + 24 + 8 * w, 8), :] = rounded[at : at + 8]
            at += 8


def kernel_body(
    src_ref,
    sea_ref,
    cot_ref,
    k_ref,
    cb_ref,
    gain_ref,
    lnb_ref,
    win_ref,
    bin_ref,
    wout_ref,
    bout_ref,
    ls_ref,
    out_ref,
    gf_ref,
    gk_ref,
    gcb_ref,
    ggain_ref,
    glnb_ref,
    gwin_ref,
    gbin_ref,
    gwout_ref,
    gbout_ref,
    gls_ref,
    q,
    qg,
    field,
    up_field,
    nat,
    taps,
    corner,
    tap_acc,
    acc_win,
    acc_wout,
    acc_bin,
    acc_vec,
    frames,
    held_in,
    held_grad,
    chosen,
    halos,
    buf,
    other,
    pieces,
    part,
    line,
    total,
    small,
    small_other,
    small_line,
    small_part,
    small_plane,
    small_total,
    ex_sent,
    ex_landed,
    sent,
    landed,
):
    t, d = lax.axis_index("tiles"), lax.axis_index("dp")
    x, zl, y = lax.div(t, 16), lax.rem(lax.div(t, 4), 4), lax.rem(t, 4)
    zh, core = lax.div(d, 2), lax.rem(d, 2)
    plane, z = 4 * x + y, 4 * zh + zl

    def in_plane(o):
        there = lax.rem(plane + o, 16)
        return there, {"tiles": 16 * lax.div(there, 4) + 4 * zl + lax.rem(there, 4), "dp": d}

    def in_line(o):
        there = lax.rem(z + o, 8)
        return there, {"tiles": 16 * x + 4 * lax.rem(there, 4) + y, "dp": 2 * lax.div(there, 4) + core}

    def in_tiles(o):
        there = lax.rem(t + o, NT)
        return there, {"tiles": there, "dp": d}

    twin = {"tiles": t, "dp": 2 * zh + (1 - core)}

    def send(src, dst, send_sem, recv_sem, device):
        copy = pltpu.make_async_remote_copy(
            src_ref=src,
            dst_ref=dst,
            send_sem=send_sem,
            recv_sem=recv_sem,
            device_id=device,
            device_id_type=MESH,
        )
        copy.start()
        return copy

    barrier = pltpu.get_barrier_semaphore()

    def greet(device):
        pl.semaphore_signal(barrier, inc=1, device_id=device, device_id_type=MESH)

    loop(1, NT, lambda o: greet(in_tiles(o)[1]))
    greet(twin)
    loop(0, 4, lambda n: greet({"tiles": 16 * x + 4 * n + y, "dp": 2 * (1 - zh) + core}))

    held = (held_in, held_grad)

    def spread(n):
        def one(o):
            chunk, device = in_tiles(o)

            @pl.when(chunk < NCH)
            def _():
                send(frames.at[n, chunk], held[n].at[t], ex_sent.at[n, 0], ex_landed.at[n, 0], device)

        held[n][NT] = jnp.zeros((16, C), BF16)
        loop(1, NT, one)

    def hand_on(n):
        @pl.when(t < NCH)
        def _():
            held[n][t] = frames[n, t]
            wait_bytes(held[n], NT - 1, ex_landed.at[n, 0])

            def one(o):
                to, device = in_tiles(o)
                chosen[n, to] = held[n][src_ref[to]]
                send(chosen.at[n, to], halos.at[n, t], ex_sent.at[n, 1], ex_landed.at[n, 1], device)

            loop(1, NT, one)
            halos[n, t] = held[n][src_ref[t]]

    def collect(n):
        @pl.when(t < NCH)
        def _():
            wait_bytes(halos.at[n], NCH - 1, ex_landed.at[n, 1])
            wait_bytes(held[n], NCH - 1, ex_sent.at[n, 0])
            wait_bytes(held[n], NT - 1, ex_sent.at[n, 1])

        @pl.when(t >= NCH)
        def _():
            wait_bytes(halos.at[n], NCH, ex_landed.at[n, 1])
            wait_bytes(held[n], NCH, ex_sent.at[n, 0])

    def deal_input(p):
        nat[rows(aligned(p * T), T), :] = sea_ref[p].astype(F32)
        for w in range(8):
            q[rows(aligned((p + 3) * QROW + 24 + 8 * w), 8), :] = nat[rows(p * T + w, 8, 8), :]
        margins(q, p + 3)

    def no_rows(q):
        for first in (0, 67 * QROW):
            q[rows(first, 3 * QROW), :] = jnp.zeros((3 * QROW, C), F32)

    no_rows(q)
    no_rows(qg)
    loop(0, T, deal_input)
    pack(q, frames.at[0], corner)
    for i in range(7):
        for j in range(7):
            taps[7 * i + j] = jnp.broadcast_to(k_ref[i, pl.ds(j, 1), :], (8, C))
    pl.semaphore_wait(barrier, NT - 1 + 5)
    spread(0)

    def deal_cotangent(p):
        nat[rows(aligned(p * T), T), :] = cot_ref[p].astype(F32)
        for w in range(8):
            up_field[rows(aligned(WPOS[w] * 512 + 8 * p), 8), :] = nat[rows(p * T + w, 8, 8), :]

    loop(0, T, deal_cotangent)
    for acc in (acc_win, acc_wout, acc_bin, acc_vec, tap_acc):
        acc[...] = jnp.zeros_like(acc)
    loop(0, 8, lambda group: convolve(q, taps, field, group, False))
    hand_on(0)

    weights = (cb_ref, gain_ref, lnb_ref, win_ref, bin_ref, wout_ref, bout_ref, ls_ref)
    sums = (acc_win, acc_wout, acc_bin, acc_vec)
    pointwise(BLOCKS[0], field, up_field, weights, nat, qg, sums)
    collect(0)
    neighbours_in(q, halos.at[0], corner, taps, field, False)
    for runs in BLOCKS[1:]:
        pointwise(runs, field, up_field, weights, nat, qg, sums)

    for n in range(4):
        block = pl.ds(n * C, C)
        buf[block, :] = acc_win[:, block]
        buf[pl.ds(512 + n * C, C), :] = acc_wout[:, block].T
    mine = pl.multiple_of(core * HALF, HALF)
    yours = pl.multiple_of((1 - core) * HALF, HALF)
    to_twin = send(buf.at[pl.ds(yours, HALF)], other, sent.at[0], landed.at[0], twin)
    loop(3, 3 + T, lambda row: margins(qg, row))
    pack(qg, frames.at[1], corner)
    spread(1)

    loop(0, T // 2, lambda p: tap_sums(q, qg, tap_acc, p))

    to_twin.wait()
    other[...] = other[...] + buf[pl.ds(mine, HALF), :]

    def scatter(o):
        there, device = in_plane(o)
        at = pl.multiple_of(there * PIECE, PIECE)
        send(other.at[pl.ds(at, PIECE)], pieces.at[plane], sent.at[1], landed.at[1], device)

    loop(1, 16, scatter)
    here = pl.multiple_of(plane * PIECE, PIECE)
    pieces[plane] = other[pl.ds(here, PIECE), :]
    hand_on(1)

    loop(T // 2, T, lambda p: tap_sums(q, qg, tap_acc, p))
    for n in range(49):
        small[rows(n, 1), :] = jnp.sum(tap_acc[n], 0, keepdims=True)
    for n in range(4):
        small[rows(49 + n, 1), :] = jnp.sum(acc_bin[:, pl.ds(n * C, C)], 0, keepdims=True)
    for n in range(5):
        small[rows(53 + n, 1), :] = jnp.sum(acc_vec[n], 0, keepdims=True)
    small[rows(58, 6), :] = jnp.zeros((6, C), F32)
    small_to_twin = send(small, small_other, sent.at[5], landed.at[5], twin)

    loop(0, 4, lambda group: convolve(qg, taps, field, group, True))

    wait_bytes(pieces, 15, landed.at[1])
    part[...] = jnp.sum(pieces[...], 0)
    loop(1, 8, lambda o: send(part, line.at[z], sent.at[2], landed.at[2], in_line(o)[1]) and None)
    line[z] = part[...]

    small_to_twin.wait()
    small[...] = small[...] + small_other[...]

    def small_scatter(o):
        there, device = in_line(o)
        at = pl.multiple_of(there * 8, 8)
        send(small.at[pl.ds(at, 8)], small_line.at[z], sent.at[6], landed.at[6], device)

    loop(1, 8, small_scatter)
    my_small = pl.multiple_of(z * 8, 8)
    small_line[z] = small[pl.ds(my_small, 8), :]

    loop(4, 8, lambda group: convolve(qg, taps, field, group, True))

    wait_bytes(line, 7, landed.at[2])
    my_piece = pl.multiple_of(mine + here, PIECE)
    total[pl.ds(my_piece, PIECE), :] = jnp.sum(line[...], 0) * SCALE

    def gather(o):
        spot = total.at[pl.ds(my_piece, PIECE)]
        send(spot, spot, sent.at[3], landed.at[3], in_plane(o)[1])

    loop(1, 16, gather)

    wait_bytes(small_line, 7, landed.at[6])
    small_part[...] = jnp.sum(small_line[...], 0)
    loop(
        1,
        16,
        lambda o: send(small_part, small_plane.at[plane], sent.at[7], landed.at[7], in_plane(o)[1]) and None,
    )
    small_plane[plane] = small_part[...]

    collect(1)
    neighbours_in(qg, halos.at[1], corner, taps, field, True)

    wait_bytes(small_plane, 15, landed.at[7])
    small_total[pl.ds(my_small, 8), :] = jnp.sum(small_plane[...], 0) * SCALE

    def small_gather(o):
        spot = small_total.at[pl.ds(my_small, 8)]
        send(spot, spot, sent.at[8], landed.at[8], in_line(o)[1])

    loop(1, 8, small_gather)
    wait_bytes(pieces, 15, landed.at[3])
    half = total.at[pl.ds(mine, HALF)]
    last = send(half, half, sent.at[4], landed.at[4], twin)

    def write_out(p):
        at = aligned(p * T)
        out_ref[p] = (sea_ref[p].astype(F32) + nat[rows(at, T), :]).astype(BF16)
        for w in range(8):
            nat[rows(p * T + w, 8, 8), :] = field[rows(aligned(WPOS[w] * 512 + 8 * p), 8), :]
        gf_ref[p] = (cot_ref[p].astype(F32) + nat[rows(at, T), :]).astype(BF16)

    loop(0, T, write_out)

    wait_bytes(small_line, 7, landed.at[8])
    for i in range(7):
        gk_ref[i] = small_total[rows(7 * i, 7), :]
    for n in range(4):
        gbin_ref[:, pl.ds(n * C, C)] = small_total[rows(49 + n, 1), :]
    for n, ref in enumerate((gcb_ref, ggain_ref, glnb_ref, gbout_ref, gls_ref)):
        ref[...] = small_total[rows(53 + n, 1), :]
    last.wait()
    for n in range(4):
        block = pl.ds(n * C, C)
        gwin_ref[:, block] = total[block, :]
    gwout_ref[...] = total[pl.ds(512, 512), :]

    wait_bytes(pieces, 15, sent.at[1])
    wait_bytes(line, 7, sent.at[2])
    wait_bytes(pieces, 15, sent.at[3])
    wait_bytes(small_line, 7, sent.at[6])
    wait_bytes(small_plane, 15, sent.at[7])
    wait_bytes(small_line, 7, sent.at[8])


def whole_block(src, sea, cot, kernel, conv_bias, ln_gain, ln_bias, w_in, b_in, w_out, b_out, layer_scale):
    vmem = pl.BlockSpec(memory_space=pltpu.VMEM)
    vec = jax.ShapeDtypeStruct((1, C), F32)
    f32 = lambda *shape: pltpu.VMEM(shape, F32)
    bf16 = lambda *shape: pltpu.VMEM(shape, BF16)
    return pl.pallas_call(
        kernel_body,
        out_shape=(
            jax.ShapeDtypeStruct((T, T, C), BF16),
            jax.ShapeDtypeStruct((T, T, C), BF16),
            jax.ShapeDtypeStruct((7, 7, C), F32),
            vec,
            vec,
            vec,
            jax.ShapeDtypeStruct((C, HID), F32),
            jax.ShapeDtypeStruct((1, HID), F32),
            jax.ShapeDtypeStruct((HID, C), F32),
            vec,
            vec,
        ),
        in_specs=[pl.BlockSpec(memory_space=pltpu.SMEM)] + [vmem] * 11,
        out_specs=(vmem,) * 11,
        scratch_shapes=[
            f32(PW * QROW, C),
            f32(PW * QROW, C),
            f32(T * T, C),
            f32(T * T, C),
            f32(T * T, C),
            f32(49, 8, C),
            f32(16, C),
            f32(49, 8, C),
            f32(C, HID),
            f32(C, HID),
            f32(8, HID),
            f32(5, 8, C),
            bf16(2, NCH, 16, C),
            bf16(NT + 1, 16, C),
            bf16(NT + 1, 16, C),
            bf16(2, NT, 16, C),
            bf16(2, NCH, 16, C),
            f32(ALL_ROWS, C),
            f32(HALF, C),
            f32(16, PIECE, C),
            f32(PIECE, C),
            f32(8, PIECE, C),
            f32(ALL_ROWS, C),
            f32(SMALL, C),
            f32(SMALL, C),
            f32(8, 8, C),
            f32(8, C),
            f32(16, 8, C),
            f32(SMALL, C),
            pltpu.SemaphoreType.DMA((2, 2)),
            pltpu.SemaphoreType.DMA((2, 2)),
            pltpu.SemaphoreType.DMA((9,)),
            pltpu.SemaphoreType.DMA((9,)),
        ],
        compiler_params=pltpu.CompilerParams(
            collective_id=1, has_side_effects=True, vmem_limit_bytes=VMEM_LIMIT
        ),
        name="whole_block",
    )(
        src,
        sea,
        cot,
        kernel,
        conv_bias.reshape(1, C),
        ln_gain.reshape(1, C),
        ln_bias.reshape(1, C),
        w_in,
        b_in.reshape(1, HID),
        w_out,
        b_out.reshape(1, C),
        layer_scale.reshape(1, C),
    )


def sources(tile_deal, adjacency):
    me = lax.axis_index("tiles")
    way = jnp.where(me < 48, lax.div(me, 12), lax.rem(me, 4) + 4)
    ids = jnp.arange(NT, dtype=jnp.int32)
    picked = jnp.sum(jnp.where(jnp.arange(8)[None, :] == way, adjacency, 0), 1)
    near = jnp.sum(jnp.where(tile_deal[:, None] == ids[None, :], picked[None, :], 0), 1)
    holder = jnp.sum(jnp.where(near[:, None] == tile_deal[None, :], ids[None, :], 0), 1)
    return jnp.where(near < 0, NT, holder).astype(jnp.int32)


def on_device(
    sea_state,
    cotangent,
    kernel,
    conv_bias,
    ln_gain,
    ln_bias,
    w_in,
    b_in,
    w_out,
    b_out,
    layer_scale,
    tile_deal,
    adjacency,
):
    src = sources(tile_deal, adjacency)
    out, gf, gk, gcb, ggain, glnb, gwin, gbin, gwout, gbout, gls = whole_block(
        src,
        sea_state[0, 0],
        cotangent[0, 0],
        kernel,
        conv_bias,
        ln_gain,
        ln_bias,
        w_in,
        b_in,
        w_out,
        b_out,
        layer_scale,
    )
    return (
        out[None, None],
        gf[None, None],
        gk,
        gcb.reshape(C),
        ggain.reshape(C),
        glnb.reshape(C),
        gwin,
        gbin.reshape(HID),
        gwout,
        gbout.reshape(C),
        gls.reshape(C),
    )


def solution(mesh):
    field = P("dp", "tiles", None, None, None)
    return jax.shard_map(
        on_device,
        mesh=mesh,
        in_specs=(field, field) + (P(),) * 11,
        out_specs=(field, field) + (P(),) * 9,
        check_vma=False,
    )
```

time: 1200 us -> 83.5 us (0.07)
  the two profiles are of different devices: /device:TPU:8 before, /device:TPU:1 now
where the time goes in v2:
time: 83.5 us; the launch traced here: 82 us
  Pallas kernels  70.1 us (84%)
  local copies, waits for them, and re-layouts  10.2 us (12%)
  other arithmetic  0.97 us (1%)
    pallas_call x1, Pallas kernels, whole_block(): pl.pallas_call(kernel_body, out_shape=(jax.ShapeDtypeStruct((T, T, C), BF...  70.1 us
    unnamed x35, local copies, waits for them, and re-layouts  10.2 us

profile of v2, /device:TPU:1, one launch (start us, length us, event | category | flops | bytes accessed | tf_op | source)
XLA Modules:
  0.0 82.0 jit_solution(13757424608446680276)
XLA Ops:
  0.6 0.0 copy-start.4
  0.7 0.7 copy-done.4
  1.3 0.0 copy-start.6
  1.3 0.1 select_reduce_fusion.2
  1.4 0.6 copy-done.6
  2.0 0.2 select_reduce_fusion.1
  2.2 0.2 select_reduce_fusion
  2.4 0.5 compare_select_fusion.src_ref
  2.9 70.1 %whole_block.1 = (bf16[64,64,128]{2,1,0:T(8,128)(2,1)}, bf16[64,64,128]{2,1,0:T(8,128)(2,1)}, f32[7,7,128]{2,1,0:T(8,128)}, f32[1,128]{1,0:T(1,128)}, f32[1,128]...) custom-call(s32[64]{0:T(128)} %compare_select_fusion.src_ref, ...), custom_call_target="tpu_custom_call" | custom-call | tf_op jit(solution)/shard_map/whole_block/pallas_call | solution.py:543
  73.0 0.0 copy-start
  73.0 2.4 %copy.35 = bf16[1,1,64,64,128]{4,3,2,1,0:T(8,128)(2,1)} copy(bf16[1,1,64,64,128]{4,3,2,1,0:T(8,128)(2,1)} %bitcast.19) | data formatting | bytes 2097152
  75.4 0.0 copy-done
  75.4 0.0 copy-start.3
  75.4 0.0 copy-start.2
  75.4 1.0 %copy.36 = bf16[1,1,64,64,128]{4,3,2,1,0:T(8,128)(2,1)} copy(bf16[1,1,64,64,128]{4,3,2,1,0:T(8,128)(2,1)S(1)} %bitcast.18) | data formatting | bytes 2097152
  76.3 0.0 copy-done.3
  76.3 0.0 copy-start.11
  76.3 0.6 copy.37
  76.9 0.1 copy-done.11
  77.0 0.0 copy-start.10
  77.0 0.5 copy.38
  77.5 0.1 copy-done.10
  77.6 0.0 copy-start.9
  77.6 0.5 copy.39
  78.1 0.2 copy-done.9
  78.3 0.5 copy.40
  78.8 0.0 copy-done.2
  78.8 0.0 copy-start.5
  78.8 0.0 copy-start.1
  78.8 0.7 copy.41
  79.5 0.0 copy-done.5
  79.5 0.6 copy.42
  80.1 0.0 copy-done.1
  80.1 0.0 copy-start.8
  80.1 0.7 copy.43
  80.8 0.0 copy-done.8
  80.8 0.0 copy-start.7
  80.8 0.5 copy.44
  81.3 0.1 copy-done.7
  81.4 0.5 copy.45
  (1 shorter events, 0.0 us)
Async XLA Ops:
  0.6 0.7 copy-start.4
  1.3 0.7 copy-start.6
  73.0 2.4 %copy-start = (bf16[64,64,128]{2,1,0:T(8,128)(2,1)S(1)}, bf16[64,64,128]{2,1,0:T(8,128)(2,1)}, u32[]{:S(2)}) copy-start(bf16[64,64,128]{2,1,0:T(8,128)(2,1)} %get-tuple-element.23) | copy-start | bytes 3145732
  75.4 1.0 %copy-start.3 = (f32[7,7,128]{2,1,0:T(8,128)S(1)}, f32[7,7,128]{2,1,0:T(8,128)}, u32[]{:S(2)}) copy-start(f32[7,7,128]{2,1,0:T(8,128)} %get-tuple-element.46) | copy-start | bytes 75268
  75.4 3.4 %copy-start.2 = (f32[128,512]{1,0:T(8,128)S(1)}, f32[128,512]{1,0:T(8,128)}, u32[]{:S(2)}) copy-start(f32[128,512]{1,0:T(8,128)} %get-tuple-element.50) | copy-start | bytes 786436
  76.3 0.7 copy-start.11
  77.0 0.6 copy-start.10
  77.6 0.7 copy-start.9
  78.8 0.7 copy-start.5
  78.8 1.3 %copy-start.1 = (f32[512,128]{1,0:T(8,128)S(1)}, f32[512,128]{1,0:T(8,128)}, u32[]{:S(2)}) copy-start(f32[512,128]{1,0:T(8,128)} %get-tuple-element.52) | copy-start | bytes 786436
  80.1 0.7 copy-start.8
  80.8 0.6 copy-start.7

commit v3 on v2

--- a/solution.py
+++ b/solution.py
@@ -22,14 +22,10 @@
 
 QROW = 14 * 8
 WPOS = (6, 4, 2, 0, 1, 3, 5, 7)
-WOF = tuple(WPOS.index(n) for n in range(8))
-BLOCKS = (
-    ((1, 7), (9, 15)),
-    ((0, 1), (7, 9), (15, 24)),
-    ((24, 36),),
-    ((36, 48),),
-    ((48, 64),),
-)
+EDGE_ROWS = (0, 1, 2, 61, 62, 63)
+EDGE_COLS = ((0, 0), (1, 0), (2, 0), (5, 7), (6, 7), (7, 7))
+BORDER = 768
+BLOCK = 1024
 
 ALL_ROWS = 1024
 HALF = ALL_ROWS // 2
@@ -184,16 +180,10 @@
     return lax.dot_general(a, b, (contract, ((), ())), preferred_element_type=F32)
 
 
-def pointwise(runs, field, up_field, weights, nat, qg, sums):
+def pointwise(convolved, up, weights, sums):
     cb_ref, gain_ref, lnb_ref, win_ref, bin_ref, wout_ref, bout_ref, ls_ref = weights
     acc_win, acc_wout, acc_bin, acc_vec = sums
-
-    def take(ref):
-        parts = [ref[rows(a * 64, (b - a) * 64), :] for a, b in runs]
-        return parts[0] if len(parts) == 1 else jnp.concatenate(parts, 0)
-
-    convolved = take(field) + cb_ref[...]
-    up = take(up_field)
+    convolved = convolved + cb_ref[...]
     centred = convolved - jnp.mean(convolved, -1, keepdims=True)
     inv_std = lax.rsqrt(jnp.mean(centred * centred, -1, keepdims=True) + 1e-06)
     whitened = centred * inv_std
@@ -227,15 +217,33 @@
     acc_vec[2] += fold(grad_normed)
     acc_vec[3] += fold(grad_out)
     acc_vec[4] += fold(up * branch)
-    scaled = branch * ls_ref[...]
-    rounded = grad_conv.astype(BF16).astype(F32)
-    at = 0
-    for a, b in runs:
-        for n in range(8 * a, 8 * b):
-            w, p = WOF[n // 64], n % 64
+    return branch * ls_ref[...], grad_conv.astype(BF16).astype(F32)
+
+
+def tile_block(b, field, up_field, weights, sums, nat, qg):
+    spot = rows(pl.multiple_of(b * BLOCK, BLOCK), BLOCK)
+    scaled, rounded = pointwise(field[spot, :], up_field[spot, :], weights, sums)
+    for n, w in enumerate((3 - b, 4 + b)):
+        for p in range(T):
+            at = 512 * n + 8 * p
+            nat[rows(p * T + w, 8, 8), :] = scaled[at : at + 8]
+            qg[rows(aligned((p + 3) * QROW + 24 + 8 * w), 8), :] = rounded[at : at + 8]
+
+
+def border_block(field, border_up, weights, sums, nat, qg):
+    parts = [field[rows(WPOS[w] * 512 + 8 * p, 8), :] for p in EDGE_ROWS for w in range(8)]
+    parts += [field[rows(WPOS[w] * 512 + 64 * n + s, 8, 8), :] for w, s in EDGE_COLS for n in range(8)]
+    scaled, rounded = pointwise(jnp.concatenate(parts, 0), border_up[...], weights, sums)
+    for e, (w, s) in enumerate(EDGE_COLS):
+        for n in range(8):
+            at = 384 + 64 * e + 8 * n
+            nat[rows(8 * n * T + 8 * s + w, 8, T), :] = scaled[at : at + 8]
+            qg[rows((8 * n + 3) * QROW + 24 + 8 * w + s, 8, QROW), :] = rounded[at : at + 8]
+    for e, p in enumerate(EDGE_ROWS):
+        for w in range(8):
+            at = 64 * e + 8 * w
             nat[rows(p * T + w, 8, 8), :] = scaled[at : at + 8]
             qg[rows((p + 3) * QROW + 24 + 8 * w, 8), :] = rounded[at : at + 8]
-            at += 8
 
 
 def kernel_body(
@@ -266,6 +274,7 @@
     qg,
     field,
     up_field,
+    border_up,
     nat,
     taps,
     corner,
@@ -395,12 +404,33 @@
     pl.semaphore_wait(barrier, NT - 1 + 5)
     spread(0)
 
+    lane = lax.broadcasted_iota(jnp.int32, (8, C), 0)
+
     def deal_cotangent(p):
         nat[rows(aligned(p * T), T), :] = cot_ref[p].astype(F32)
         for w in range(8):
-            up_field[rows(aligned(WPOS[w] * 512 + 8 * p), 8), :] = nat[rows(p * T + w, 8, 8), :]
+            cells = nat[rows(p * T + w, 8, 8), :]
+            if w < 3:
+                cells = jnp.where(lane == 0, 0.0, cells)
+            if w > 4:
+                cells = jnp.where(lane == 7, 0.0, cells)
+            up_field[rows(aligned(WPOS[w] * 512 + 8 * p), 8), :] = cells
 
     loop(0, T, deal_cotangent)
+    for w in range(8):
+        for first in (0, 61):
+            up_field[rows(WPOS[w] * 512 + 8 * first, 24), :] = jnp.zeros((24, C), F32)
+    for e, p in enumerate(EDGE_ROWS):
+        for w in range(8):
+            border_up[rows(64 * e + 8 * w, 8), :] = nat[rows(p * T + w, 8, 8), :]
+    for e, (w, s) in enumerate(EDGE_COLS):
+        for n in range(8):
+            cells = nat[rows(8 * n * T + 8 * s + w, 8, T), :]
+            if n == 0:
+                cells = jnp.where(lane < 3, 0.0, cells)
+            if n == 7:
+                cells = jnp.where(lane > 4, 0.0, cells)
+            border_up[rows(384 + 64 * e + 8 * n, 8), :] = cells
     for acc in (acc_win, acc_wout, acc_bin, acc_vec, tap_acc):
         acc[...] = jnp.zeros_like(acc)
     loop(0, 8, lambda group: convolve(q, taps, field, group, False))
@@ -408,11 +438,10 @@
 
     weights = (cb_ref, gain_ref, lnb_ref, win_ref, bin_ref, wout_ref, bout_ref, ls_ref)
     sums = (acc_win, acc_wout, acc_bin, acc_vec)
-    pointwise(BLOCKS[0], field, up_field, weights, nat, qg, sums)
+    loop(0, 4, lambda b: tile_block(b, field, up_field, weights, sums, nat, qg))
     collect(0)
     neighbours_in(q, halos.at[0], corner, taps, field, False)
-    for runs in BLOCKS[1:]:
-        pointwise(runs, field, up_field, weights, nat, qg, sums)
+    border_block(field, border_up, weights, sums, nat, qg)
 
     for n in range(4):
         block = pl.ds(n * C, C)
@@ -421,11 +450,17 @@
     mine = pl.multiple_of(core * HALF, HALF)
     yours = pl.multiple_of((1 - core) * HALF, HALF)
     to_twin = send(buf.at[pl.ds(yours, HALF)], other, sent.at[0], landed.at[0], twin)
-    loop(3, 3 + T, lambda row: margins(qg, row))
     pack(qg, frames.at[1], corner)
     spread(1)
-
-    loop(0, T // 2, lambda p: tap_sums(q, qg, tap_acc, p))
+    loop(3, 3 + T, lambda row: margins(qg, row))
+
+    def tap_rows(first, last):
+        loop(first, last, lambda p: tap_sums(q, qg, tap_acc, p))
+
+    def back_rows(first, last):
+        loop(first, last, lambda group: convolve(qg, taps, field, group, True))
+
+    tap_rows(0, 16)
 
     to_twin.wait()
     other[...] = other[...] + buf[pl.ds(mine, HALF), :]
@@ -438,9 +473,8 @@
     loop(1, 16, scatter)
     here = pl.multiple_of(plane * PIECE, PIECE)
     pieces[plane] = other[pl.ds(here, PIECE), :]
-    hand_on(1)
-
-    loop(T // 2, T, lambda p: tap_sums(q, qg, tap_acc, p))
+
+    tap_rows(16, T)
     for n in range(49):
         small[rows(n, 1), :] = jnp.sum(tap_acc[n], 0, keepdims=True)
     for n in range(4):
@@ -449,8 +483,9 @@
         small[rows(53 + n, 1), :] = jnp.sum(acc_vec[n], 0, keepdims=True)
     small[rows(58, 6), :] = jnp.zeros((6, C), F32)
     small_to_twin = send(small, small_other, sent.at[5], landed.at[5], twin)
-
-    loop(0, 4, lambda group: convolve(qg, taps, field, group, True))
+    hand_on(1)
+
+    back_rows(0, 1)
 
     wait_bytes(pieces, 15, landed.at[1])
     part[...] = jnp.sum(pieces[...], 0)
@@ -469,17 +504,7 @@
     my_small = pl.multiple_of(z * 8, 8)
     small_line[z] = small[pl.ds(my_small, 8), :]
 
-    loop(4, 8, lambda group: convolve(qg, taps, field, group, True))
-
-    wait_bytes(line, 7, landed.at[2])
-    my_piece = pl.multiple_of(mine + here, PIECE)
-    total[pl.ds(my_piece, PIECE), :] = jnp.sum(line[...], 0) * SCALE
-
-    def gather(o):
-        spot = total.at[pl.ds(my_piece, PIECE)]
-        send(spot, spot, sent.at[3], landed.at[3], in_plane(o)[1])
-
-    loop(1, 16, gather)
+    back_rows(1, 5)
 
     wait_bytes(small_line, 7, landed.at[6])
     small_part[...] = jnp.sum(small_line[...], 0)
@@ -490,8 +515,19 @@
     )
     small_plane[plane] = small_part[...]
 
-    collect(1)
-    neighbours_in(qg, halos.at[1], corner, taps, field, True)
+    back_rows(5, 6)
+
+    wait_bytes(line, 7, landed.at[2])
+    my_piece = pl.multiple_of(mine + here, PIECE)
+    total[pl.ds(my_piece, PIECE), :] = (jnp.sum(line[...], 0) * SCALE).astype(BF16)
+
+    def gather(o):
+        spot = total.at[pl.ds(my_piece, PIECE)]
+        send(spot, spot, sent.at[3], landed.at[3], in_plane(o)[1])
+
+    loop(1, 16, gather)
+
+    back_rows(6, 8)
 
     wait_bytes(small_plane, 15, landed.at[7])
     small_total[pl.ds(my_small, 8), :] = jnp.sum(small_plane[...], 0) * SCALE
@@ -501,18 +537,27 @@
         send(spot, spot, sent.at[8], landed.at[8], in_line(o)[1])
 
     loop(1, 8, small_gather)
-    wait_bytes(pieces, 15, landed.at[3])
-    half = total.at[pl.ds(mine, HALF)]
-    last = send(half, half, sent.at[4], landed.at[4], twin)
 
     def write_out(p):
         at = aligned(p * T)
         out_ref[p] = (sea_ref[p].astype(F32) + nat[rows(at, T), :]).astype(BF16)
+
+    loop(0, T, write_out)
+
+    gathered = total.at[pl.ds(0, 15 * PIECE)]
+    pltpu.make_async_copy(gathered, gathered, landed.at[3]).wait()
+    half = total.at[pl.ds(mine, HALF)]
+    last = send(half, half, sent.at[4], landed.at[4], twin)
+
+    collect(1)
+    neighbours_in(qg, halos.at[1], corner, taps, field, True)
+
+    def write_grad(p):
         for w in range(8):
             nat[rows(p * T + w, 8, 8), :] = field[rows(aligned(WPOS[w] * 512 + 8 * p), 8), :]
-        gf_ref[p] = (cot_ref[p].astype(F32) + nat[rows(at, T), :]).astype(BF16)
-
-    loop(0, T, write_out)
+        gf_ref[p] = (cot_ref[p].astype(F32) + nat[rows(aligned(p * T), T), :]).astype(BF16)
+
+    loop(0, T, write_grad)
 
     wait_bytes(small_line, 7, landed.at[8])
     for i in range(7):
@@ -524,12 +569,12 @@
     last.wait()
     for n in range(4):
         block = pl.ds(n * C, C)
-        gwin_ref[:, block] = total[block, :]
-    gwout_ref[...] = total[pl.ds(512, 512), :]
+        gwin_ref[:, block] = total[block, :].astype(F32)
+    gwout_ref[...] = total[pl.ds(512, 512), :].astype(F32)
 
     wait_bytes(pieces, 15, sent.at[1])
     wait_bytes(line, 7, sent.at[2])
-    wait_bytes(pieces, 15, sent.at[3])
+    pltpu.make_async_copy(gathered, gathered, sent.at[3]).wait()
     wait_bytes(small_line, 7, sent.at[6])
     wait_bytes(small_plane, 15, sent.at[7])
     wait_bytes(small_line, 7, sent.at[8])
@@ -562,6 +607,7 @@
             f32(PW * QROW, C),
             f32(T * T, C),
             f32(T * T, C),
+            f32(BORDER, C),
             f32(T * T, C),
             f32(49, 8, C),
             f32(16, C),
@@ -580,7 +626,7 @@
             f32(16, PIECE, C),
             f32(PIECE, C),
             f32(8, PIECE, C),
-            f32(ALL_ROWS, C),
+            bf16(ALL_ROWS, C),
             f32(SMALL, C),
             f32(SMALL, C),
             f32(8, 8, C),
@@ -610,6 +656,45 @@
         b_out.reshape(1, C),
         layer_scale.reshape(1, C),
     )
+
+
+HAND_ROWS = 16
+
+
+def hand_over_kernel(*refs):
+    count = (len(refs) - 2) // 3
+    here, there = refs[-2:]
+    parts = []
+    for n in range(count):
+        a, b, mid = refs[n], refs[count + n], refs[2 * count + n]
+        if a.shape[0] == T:
+            for first in range(0, T, HAND_ROWS):
+                parts.append([r.at[pl.ds(first, HAND_ROWS)] for r in (a, mid, b)])
+        else:
+            parts.append([a, mid, b])
+    arrive = [pltpu.make_async_copy(a, mid, here.at[n]) for n, (a, mid, _) in enumerate(parts)]
+    leave = [pltpu.make_async_copy(mid, b, there.at[n]) for n, (_, mid, b) in enumerate(parts)]
+    for copy in arrive:
+        copy.start()
+    for first, then in zip(arrive, leave):
+        first.wait()
+        then.start()
+    for copy in leave:
+        copy.wait()
+
+
+def hand_over(*arrays):
+    anywhere = pl.BlockSpec(memory_space=pl.ANY)
+    parts = len(arrays) + sum(T // HAND_ROWS - 1 for a in arrays if a.shape[0] == T)
+    return pl.pallas_call(
+        hand_over_kernel,
+        out_shape=tuple(jax.ShapeDtypeStruct(a.shape, a.dtype) for a in arrays),
+        in_specs=[anywhere] * len(arrays),
+        out_specs=(anywhere,) * len(arrays),
+        scratch_shapes=[pltpu.VMEM(a.shape, a.dtype) for a in arrays]
+        + [pltpu.SemaphoreType.DMA((parts,)), pltpu.SemaphoreType.DMA((parts,))],
+        name="hand_over",
+    )(*arrays)
 
 
 def sources(tile_deal, adjacency):
@@ -652,6 +737,9 @@
         b_out,
         layer_scale,
     )
+    out, gf, gk, gcb, ggain, glnb, gwin, gbin, gwout, gbout, gls = hand_over(
+        out, gf, gk, gcb, ggain, glnb, gwin, gbin, gwout, gbout, gls
+    )
     return (
         out[None, None],
         gf[None, None],

time: 83.5 us -> 73.2 us (0.88)
  local copies, waits for them, and re-layouts: 10.2 us -> 1.23 us
    unnamed x35 -> x4, local copies, waits for them, and re-layouts: 10.2 us -> 1.23 us
    pallas_call x1, Pallas kernels: 70.1 us -> 66.6 us  [whole_block(): pl.pallas_call(kernel_body, out_shape=(jax.ShapeDtypeStruct((T, T, C), BF...]
    pallas_call x0 -> x1, Pallas kernels: none -> 2.77 us  [hand_over(): pl.pallas_call(hand_over_kernel, out_shape=tuple((jax.ShapeDtypeStruct(a....]
where the time goes in v3:
time: 73.2 us; the launch traced here: 72.2 us
  Pallas kernels  69.4 us (95%)
  local copies, waits for them, and re-layouts  1.23 us (2%)
  other arithmetic  0.97 us (1%)
    pallas_call x1, Pallas kernels, whole_block(): pl.pallas_call(kernel_body, out_shape=(jax.ShapeDtypeStruct((T, T, C), BF...  66.6 us
    pallas_call x1, Pallas kernels, hand_over(): pl.pallas_call(hand_over_kernel, out_shape=tuple((jax.ShapeDtypeStruct(a....  2.77 us

profile of v3, /device:TPU:1, one launch (start us, length us, event | category | flops | bytes accessed | tf_op | source)
XLA Modules:
  0.0 72.2 jit_solution(11301868871497773970)
XLA Ops:
  0.6 0.0 copy-start
  0.7 0.7 copy-done
  1.3 0.0 copy-start.1
  1.3 0.1 select_reduce_fusion.2
  1.4 0.6 copy-done.1
  2.0 0.2 select_reduce_fusion.1
  2.2 0.2 select_reduce_fusion
  2.4 0.5 compare_select_fusion.src_ref
  2.9 66.6 %whole_block.1 = (bf16[64,64,128]{2,1,0:T(8,128)(2,1)}, bf16[64,64,128]{2,1,0:T(8,128)(2,1)}, f32[7,7,128]{2,1,0:T(8,128)}, f32[1,128]{1,0:T(1,128)}, f32[1,128]...) custom-call(s32[64]{0:T(128)} %compare_select_fusion.src_ref, ...), custom_call_target="tpu_custom_call" | custom-call | tf_op jit(solution)/shard_map/whole_block/pallas_call | solution.py:588
  69.5 2.8 %hand_over.1 = (bf16[64,64,128]{2,1,0:T(8,128)(2,1)}, bf16[64,64,128]{2,1,0:T(8,128)(2,1)}, f32[7,7,128]{2,1,0:T(8,128)}, f32[1,128]{1,0:T(1,128)}, f32[1,128]{1...) custom-call(bf16[64,64,128]{2,1,0:T(8,128)(2,1)} %get-tuple-element., ...), custom_call_target="tpu_custom_call" | custom-call | tf_op jit(solution)/shard_map/hand_over/pallas_call | solution.py:689
  (1 shorter events, 0.0 us)
Async XLA Ops:
  0.6 0.7 copy-start
  1.3 0.7 copy-start.1

commit v4 on v3

--- a/solution.py
+++ b/solution.py
@@ -248,8 +248,8 @@
 
 def kernel_body(
     src_ref,
-    sea_ref,
-    cot_ref,
+    sea_hbm,
+    cot_hbm,
     k_ref,
     cb_ref,
     gain_ref,
@@ -259,8 +259,8 @@
     wout_ref,
     bout_ref,
     ls_ref,
-    out_ref,
-    gf_ref,
+    out_hbm,
+    gf_hbm,
     gk_ref,
     gcb_ref,
     ggain_ref,
@@ -290,16 +290,21 @@
     halos,
     buf,
     other,
+    paired,
     pieces,
     part,
     line,
     total,
     small,
-    small_other,
-    small_line,
+    small_column,
     small_part,
     small_plane,
     small_total,
+    sea_ref,
+    cot_ref,
+    out_ref,
+    gf_ref,
+    field_sems,
     ex_sent,
     ex_landed,
     sent,
@@ -317,6 +322,14 @@
     def in_line(o):
         there = lax.rem(z + o, 8)
         return there, {"tiles": 16 * x + 4 * lax.rem(there, 4) + y, "dp": 2 * lax.div(there, 4) + core}
+
+    def in_column(o):
+        there = lax.rem(2 * z + core + o, 16)
+        above = lax.div(there, 2)
+        return there, {
+            "tiles": 16 * x + 4 * lax.rem(above, 4) + y,
+            "dp": 2 * lax.div(above, 4) + lax.rem(there, 2),
+        }
 
     def in_tiles(o):
         there = lax.rem(t + o, NT)
@@ -336,15 +349,19 @@
         copy.start()
         return copy
 
+    sea_in = pltpu.make_async_copy(sea_hbm, sea_ref, field_sems.at[0])
+    sea_in.start()
+    cot_in = pltpu.make_async_copy(cot_hbm, cot_ref, field_sems.at[1])
+    cot_in.start()
+
     barrier = pltpu.get_barrier_semaphore()
 
     def greet(device):
         pl.semaphore_signal(barrier, inc=1, device_id=device, device_id_type=MESH)
 
     loop(1, NT, lambda o: greet(in_tiles(o)[1]))
-    greet(twin)
-    loop(0, 4, lambda n: greet({"tiles": 16 * x + 4 * n + y, "dp": 2 * (1 - zh) + core}))
-
+    for k in range(1, 4):
+        loop(0, 4, lambda n, k=k: greet({"tiles": 16 * x + 4 * n + y, "dp": lax.rem(d + k, 4)}))
     held = (held_in, held_grad)
 
     def spread(n):
@@ -396,12 +413,13 @@
 
     no_rows(q)
     no_rows(qg)
+    sea_in.wait()
     loop(0, T, deal_input)
     pack(q, frames.at[0], corner)
     for i in range(7):
         for j in range(7):
             taps[7 * i + j] = jnp.broadcast_to(k_ref[i, pl.ds(j, 1), :], (8, C))
-    pl.semaphore_wait(barrier, NT - 1 + 5)
+    pl.semaphore_wait(barrier, NT - 1 + 12)
     spread(0)
 
     lane = lax.broadcasted_iota(jnp.int32, (8, C), 0)
@@ -416,6 +434,7 @@
                 cells = jnp.where(lane == 7, 0.0, cells)
             up_field[rows(aligned(WPOS[w] * 512 + 8 * p), 8), :] = cells
 
+    cot_in.wait()
     loop(0, T, deal_cotangent)
     for w in range(8):
         for first in (0, 61):
@@ -460,21 +479,19 @@
     def back_rows(first, last):
         loop(first, last, lambda group: convolve(qg, taps, field, group, True))
 
-    tap_rows(0, 16)
-
     to_twin.wait()
-    other[...] = other[...] + buf[pl.ds(mine, HALF), :]
+    paired[...] = (other[...] + buf[pl.ds(mine, HALF), :]).astype(BF16)
 
     def scatter(o):
         there, device = in_plane(o)
         at = pl.multiple_of(there * PIECE, PIECE)
-        send(other.at[pl.ds(at, PIECE)], pieces.at[plane], sent.at[1], landed.at[1], device)
+        send(paired.at[pl.ds(at, PIECE)], pieces.at[plane], sent.at[1], landed.at[1], device)
 
     loop(1, 16, scatter)
     here = pl.multiple_of(plane * PIECE, PIECE)
-    pieces[plane] = other[pl.ds(here, PIECE), :]
-
-    tap_rows(16, T)
+    pieces[plane] = paired[pl.ds(here, PIECE), :]
+
+    tap_rows(0, T)
     for n in range(49):
         small[rows(n, 1), :] = jnp.sum(tap_acc[n], 0, keepdims=True)
     for n in range(4):
@@ -482,32 +499,28 @@
     for n in range(5):
         small[rows(53 + n, 1), :] = jnp.sum(acc_vec[n], 0, keepdims=True)
     small[rows(58, 6), :] = jnp.zeros((6, C), F32)
-    small_to_twin = send(small, small_other, sent.at[5], landed.at[5], twin)
+
+    def small_scatter(o):
+        there, device = in_column(o)
+        at = pl.multiple_of(lax.div(there, 2) * 8, 8)
+        send(small.at[pl.ds(at, 8)], small_column.at[2 * z + core], sent.at[5], landed.at[5], device)
+
+    loop(1, 16, small_scatter)
+    my_small = pl.multiple_of(z * 8, 8)
+    small_column[2 * z + core] = small[pl.ds(my_small, 8), :]
     hand_on(1)
 
     back_rows(0, 1)
 
     wait_bytes(pieces, 15, landed.at[1])
-    part[...] = jnp.sum(pieces[...], 0)
+    part[...] = jnp.sum(pieces[...].astype(F32), 0)
     loop(1, 8, lambda o: send(part, line.at[z], sent.at[2], landed.at[2], in_line(o)[1]) and None)
     line[z] = part[...]
 
-    small_to_twin.wait()
-    small[...] = small[...] + small_other[...]
-
-    def small_scatter(o):
-        there, device = in_line(o)
-        at = pl.multiple_of(there * 8, 8)
-        send(small.at[pl.ds(at, 8)], small_line.at[z], sent.at[6], landed.at[6], device)
-
-    loop(1, 8, small_scatter)
-    my_small = pl.multiple_of(z * 8, 8)
-    small_line[z] = small[pl.ds(my_small, 8), :]
-
     back_rows(1, 5)
 
-    wait_bytes(small_line, 7, landed.at[6])
-    small_part[...] = jnp.sum(small_line[...], 0)
+    wait_bytes(small_column, 15, landed.at[5])
+    small_part[...] = jnp.sum(small_column[...], 0)
     loop(
         1,
         16,
@@ -543,6 +556,8 @@
         out_ref[p] = (sea_ref[p].astype(F32) + nat[rows(at, T), :]).astype(BF16)
 
     loop(0, T, write_out)
+    out_away = pltpu.make_async_copy(out_ref, out_hbm, field_sems.at[2])
+    out_away.start()
 
     gathered = total.at[pl.ds(0, 15 * PIECE)]
     pltpu.make_async_copy(gathered, gathered, landed.at[3]).wait()
@@ -557,9 +572,14 @@
             nat[rows(p * T + w, 8, 8), :] = field[rows(aligned(WPOS[w] * 512 + 8 * p), 8), :]
         gf_ref[p] = (cot_ref[p].astype(F32) + nat[rows(aligned(p * T), T), :]).astype(BF16)
 
-    loop(0, T, write_grad)
-
-    wait_bytes(small_line, 7, landed.at[8])
+    gf_away = []
+    for n in range(2):
+        loop(32 * n, 32 * n + 32, write_grad)
+        spot = pl.ds(32 * n, 32)
+        gf_away.append(pltpu.make_async_copy(gf_ref.at[spot], gf_hbm.at[spot], field_sems.at[3 + n]))
+        gf_away[n].start()
+
+    wait_bytes(small_column, 7, landed.at[8])
     for i in range(7):
         gk_ref[i] = small_total[rows(7 * i, 7), :]
     for n in range(4):
@@ -575,13 +595,16 @@
     wait_bytes(pieces, 15, sent.at[1])
     wait_bytes(line, 7, sent.at[2])
     pltpu.make_async_copy(gathered, gathered, sent.at[3]).wait()
-    wait_bytes(small_line, 7, sent.at[6])
+    wait_bytes(small_column, 15, sent.at[5])
     wait_bytes(small_plane, 15, sent.at[7])
-    wait_bytes(small_line, 7, sent.at[8])
+    wait_bytes(small_column, 7, sent.at[8])
+    for copy in (out_away, *gf_away):
+        copy.wait()
 
 
 def whole_block(src, sea, cot, kernel, conv_bias, ln_gain, ln_bias, w_in, b_in, w_out, b_out, layer_scale):
     vmem = pl.BlockSpec(memory_space=pltpu.VMEM)
+    anywhere = pl.BlockSpec(memory_space=pl.ANY)
     vec = jax.ShapeDtypeStruct((1, C), F32)
     f32 = lambda *shape: pltpu.VMEM(shape, F32)
     bf16 = lambda *shape: pltpu.VMEM(shape, BF16)
@@ -600,8 +623,8 @@
             vec,
             vec,
         ),
-        in_specs=[pl.BlockSpec(memory_space=pltpu.SMEM)] + [vmem] * 11,
-        out_specs=(vmem,) * 11,
+        in_specs=[pl.BlockSpec(memory_space=pltpu.SMEM)] + [anywhere] * 2 + [vmem] * 9,
+        out_specs=(anywhere,) * 2 + (vmem,) * 9,
         scratch_shapes=[
             f32(PW * QROW, C),
             f32(PW * QROW, C),
@@ -623,16 +646,21 @@
             bf16(2, NCH, 16, C),
             f32(ALL_ROWS, C),
             f32(HALF, C),
-            f32(16, PIECE, C),
+            bf16(HALF, C),
+            bf16(16, PIECE, C),
             f32(PIECE, C),
             f32(8, PIECE, C),
             bf16(ALL_ROWS, C),
             f32(SMALL, C),
-            f32(SMALL, C),
-            f32(8, 8, C),
+            f32(16, 8, C),
             f32(8, C),
             f32(16, 8, C),
             f32(SMALL, C),
+            bf16(T, T, C),
+            bf16(T, T, C),
+            bf16(T, T, C),
+            bf16(T, T, C),
+            pltpu.SemaphoreType.DMA((5,)),
             pltpu.SemaphoreType.DMA((2, 2)),
             pltpu.SemaphoreType.DMA((2, 2)),
             pltpu.SemaphoreType.DMA((9,)),
@@ -722,9 +750,8 @@
     tile_deal,
     adjacency,
 ):
-    src = sources(tile_deal, adjacency)
     out, gf, gk, gcb, ggain, glnb, gwin, gbin, gwout, gbout, gls = whole_block(
-        src,
+        sources(tile_deal, adjacency),
         sea_state[0, 0],
         cotangent[0, 0],
         kernel,

time: 73.2 us -> 72 us (0.984)
  no operation moved by 1% of the time
where the time goes in v4:
time: 72 us; the launch traced here: 71.8 us
  Pallas kernels  68.9 us (96%)
  local copies, waits for them, and re-layouts  1.23 us (2%)
  other arithmetic  0.97 us (1%)
    pallas_call x1, Pallas kernels, whole_block(): pl.pallas_call(kernel_body, out_shape=(jax.ShapeDtypeStruct((T, T, C), BF...  66.1 us
    pallas_call x1, Pallas kernels, hand_over(): pl.pallas_call(hand_over_kernel, out_shape=tuple((jax.ShapeDtypeStruct(a....  2.77 us

profile of v4, /device:TPU:1, one launch (start us, length us, event | category | flops | bytes accessed | tf_op | source)
XLA Modules:
  0.0 71.8 jit_solution(12638350237697026012)
XLA Ops:
  0.6 0.0 copy-start
  0.7 0.7 copy-done
  1.3 0.0 copy-start.1
  1.3 0.1 select_reduce_fusion.2
  1.4 0.6 copy-done.1
  2.0 0.2 select_reduce_fusion.1
  2.2 0.2 select_reduce_fusion
  2.4 0.5 compare_select_fusion.src_ref
  2.9 66.1 %whole_block.1 = (bf16[64,64,128]{2,1,0:T(8,128)(2,1)}, bf16[64,64,128]{2,1,0:T(8,128)(2,1)}, f32[7,7,128]{2,1,0:T(8,128)}, f32[1,128]{1,0:T(1,128)}, f32[1,128]...) custom-call(s32[64]{0:T(128)} %compare_select_fusion.src_ref, ...), custom_call_target="tpu_custom_call" | custom-call | tf_op jit(solution)/shard_map/whole_block/pallas_call | solution.py:611
  69.0 2.8 %hand_over.1 = (bf16[64,64,128]{2,1,0:T(8,128)(2,1)}, bf16[64,64,128]{2,1,0:T(8,128)(2,1)}, f32[7,7,128]{2,1,0:T(8,128)}, f32[1,128]{1,0:T(1,128)}, f32[1,128]{1...) custom-call(bf16[64,64,128]{2,1,0:T(8,128)(2,1)} %get-tuple-element., ...), custom_call_target="tpu_custom_call" | custom-call | tf_op jit(solution)/shard_map/hand_over/pallas_call | solution.py:717
  (1 shorter events, 0.0 us)
Async XLA Ops:
  0.6 0.7 copy-start
  1.3 0.7 copy-start.1

commit v5 on v4

--- a/solution.py
+++ b/solution.py
@@ -491,7 +491,14 @@
     here = pl.multiple_of(plane * PIECE, PIECE)
     pieces[plane] = paired[pl.ds(here, PIECE), :]
 
-    tap_rows(0, T)
+    tap_rows(0, 48)
+
+    wait_bytes(pieces, 15, landed.at[1])
+    part[...] = jnp.sum(pieces[...].astype(F32), 0)
+    loop(1, 8, lambda o: send(part, line.at[z], sent.at[2], landed.at[2], in_line(o)[1]) and None)
+    line[z] = part[...]
+
+    tap_rows(48, T)
     for n in range(49):
         small[rows(n, 1), :] = jnp.sum(tap_acc[n], 0, keepdims=True)
     for n in range(4):
@@ -510,14 +517,7 @@
     small_column[2 * z + core] = small[pl.ds(my_small, 8), :]
     hand_on(1)
 
-    back_rows(0, 1)
-
-    wait_bytes(pieces, 15, landed.at[1])
-    part[...] = jnp.sum(pieces[...].astype(F32), 0)
-    loop(1, 8, lambda o: send(part, line.at[z], sent.at[2], landed.at[2], in_line(o)[1]) and None)
-    line[z] = part[...]
-
-    back_rows(1, 5)
+    back_rows(0, 3)
 
     wait_bytes(small_column, 15, landed.at[5])
     small_part[...] = jnp.sum(small_column[...], 0)
@@ -528,8 +528,6 @@
     )
     small_plane[plane] = small_part[...]
 
-    back_rows(5, 6)
-
     wait_bytes(line, 7, landed.at[2])
     my_piece = pl.multiple_of(mine + here, PIECE)
     total[pl.ds(my_piece, PIECE), :] = (jnp.sum(line[...], 0) * SCALE).astype(BF16)
@@ -540,7 +538,7 @@
 
     loop(1, 16, gather)
 
-    back_rows(6, 8)
+    back_rows(3, 8)
 
     wait_bytes(small_plane, 15, landed.at[7])
     small_total[pl.ds(my_small, 8), :] = jnp.sum(small_plane[...], 0) * SCALE
@@ -550,19 +548,19 @@
         send(spot, spot, sent.at[8], landed.at[8], in_line(o)[1])
 
     loop(1, 8, small_gather)
-
-    def write_out(p):
-        at = aligned(p * T)
-        out_ref[p] = (sea_ref[p].astype(F32) + nat[rows(at, T), :]).astype(BF16)
-
-    loop(0, T, write_out)
-    out_away = pltpu.make_async_copy(out_ref, out_hbm, field_sems.at[2])
-    out_away.start()
 
     gathered = total.at[pl.ds(0, 15 * PIECE)]
     pltpu.make_async_copy(gathered, gathered, landed.at[3]).wait()
     half = total.at[pl.ds(mine, HALF)]
     last = send(half, half, sent.at[4], landed.at[4], twin)
+
+    def write_out(p):
+        at = aligned(p * T)
+        out_ref[p] = (sea_ref[p].astype(F32) + nat[rows(at, T), :]).astype(BF16)
+
+    loop(0, T, write_out)
+    out_away = pltpu.make_async_copy(out_ref, out_hbm, field_sems.at[2])
+    out_away.start()
 
     collect(1)
     neighbours_in(qg, halos.at[1], corner, taps, field, True)

time: 72 us -> 68.6 us (0.953)
  Pallas kernels: 68.9 us -> 65.6 us
    pallas_call x1, Pallas kernels: 66.1 us -> 62.8 us  [whole_block(): pl.pallas_call(kernel_body, out_shape=(jax.ShapeDtypeStruct((T, T, C), BF...]
where the time goes in v5:
time: 68.6 us; the launch traced here: 68.4 us
  Pallas kernels  65.6 us (96%)
  local copies, waits for them, and re-layouts  1.23 us (2%)
  other arithmetic  0.97 us (1%)
  between operations  0.69 us (1%)
    pallas_call x1, Pallas kernels, whole_block(): pl.pallas_call(kernel_body, out_shape=(jax.ShapeDtypeStruct((T, T, C), BF...  62.8 us
    pallas_call x1, Pallas kernels, hand_over(): pl.pallas_call(hand_over_kernel, out_shape=tuple((jax.ShapeDtypeStruct(a....  2.77 us

profile of v5, /device:TPU:1, one launch (start us, length us, event | category | flops | bytes accessed | tf_op | source)
XLA Modules:
  0.0 68.4 jit_solution(16299221909029469728)
XLA Ops:
  0.6 0.0 copy-start
  0.7 0.7 copy-done
  1.3 0.0 copy-start.1
  1.3 0.1 select_reduce_fusion.2
  1.4 0.6 copy-done.1
  2.0 0.2 select_reduce_fusion.1
  2.2 0.2 select_reduce_fusion
  2.4 0.5 compare_select_fusion.src_ref
  2.9 62.8 %whole_block.1 = (bf16[64,64,128]{2,1,0:T(8,128)(2,1)}, bf16[64,64,128]{2,1,0:T(8,128)(2,1)}, f32[7,7,128]{2,1,0:T(8,128)}, f32[1,128]{1,0:T(1,128)}, f32[1,128]...) custom-call(s32[64]{0:T(128)} %compare_select_fusion.src_ref, ...), custom_call_target="tpu_custom_call" | custom-call | tf_op jit(solution)/shard_map/whole_block/pallas_call | solution.py:609
  65.7 2.8 %hand_over.1 = (bf16[64,64,128]{2,1,0:T(8,128)(2,1)}, bf16[64,64,128]{2,1,0:T(8,128)(2,1)}, f32[7,7,128]{2,1,0:T(8,128)}, f32[1,128]{1,0:T(1,128)}, f32[1,128]{1...) custom-call(bf16[64,64,128]{2,1,0:T(8,128)(2,1)} %get-tuple-element., ...), custom_call_target="tpu_custom_call" | custom-call | tf_op jit(solution)/shard_map/hand_over/pallas_call | solution.py:715
  (1 shorter events, 0.0 us)
Async XLA Ops:
  0.6 0.7 %copy-start = (s32[64,8]{0,1:T(8,128)S(1)}, s32[64,8]{0,1:T(8,128)}, u32[]{:S(2)}) copy-start(s32[64,8]{0,1:T(8,128)} %param.25) | copy-start | bytes 6148
  1.3 0.7 copy-start.1
